TPU v7x, 512 devices: a whole 4x8x8 slice. The times are simulated.
512 devices in a mesh: grp: 32 (over x, y), dev: 16 (over z, core).
Axes of the slice: x: 4, y: 8, z: 8, core: 2. Of those that a mesh axis runs over, the one named last changes fastest.
Arguments:
- prompt_latent_cache: bfloat16 [64, 4096, 512], P('grp', 'dev'), may hold values from -6 to 6
- prompt_rope: bfloat16 [64, 64, 4096], P('grp', None, 'dev'), may hold values from -32 to 32
- prompt_length: int32 [32, 2], P('grp'), may hold values from 256 to 4096, as said below
- dest_slot: int32 [32, 2], P('grp'), may hold values from 0 to 63, as said below
- resident_latent: bfloat16 [64, 4096, 512], P('grp', 'dev'), may hold values from -6 to 6
- resident_rope: bfloat16 [64, 64, 4096], P('grp', None, 'dev'), may hold values from -32 to 32
- resident_length: int32 [32, 2], P('grp'), may hold values from 256 to 4096, as said below
- new_latent: bfloat16 [128, 2, 512], P('grp'), may hold values from -6 to 6
- new_rope: bfloat16 [128, 2, 64], P('grp'), may hold values from -32 to 32
- query_nope: bfloat16 [128, 2, 128, 128], P('grp', None, 'dev'), may hold values from -6 to 6
- query_rope: bfloat16 [128, 2, 128, 64], P('grp', None, 'dev'), may hold values from -64 to 64
- key_up: bfloat16 [128, 128, 512], P('dev'), may hold values from -0.5 to 0.5
- value_up_weight: bfloat16 [128, 512, 128], P('dev'), may hold values from -0.25 to 0.25
Outputs:
- per_head_output: bfloat16 [128, 2, 128, 128], P('grp', None, 'dev')
Inputs may be any that keep to these rules, and one draw needn't show every extreme that they name: dest_slot[g, r] = q * 2 + c sends prompt r of prefill group g to slot c (below 2) of decode group q. All entries differ, the prompts of one prefill group go to different decode groups, and every decode group receives exactly 2 prompts. `prompt_length`: in every prefill group some prompt has exactly 4096 tokens. `resident_length`: in every decode group some resident request has exactly 4096 tokens.
All inputs are finite; a program needn't handle non-finite values.
Results may differ from a plain program's by a relative error of at most 0.0084.
Values may be sent and summed in bfloat16 or wider, within the bound.
A program may use at most 64 MiB of HBM per device.

v0:
```python
import math

import jax
import jax.numpy as jnp
from jax import lax
from jax.sharding import PartitionSpec as P


def attend_scale(nope_width, rotary_width):
    return (0.1 * math.log(40.0) + 1.0) ** 2 / math.sqrt(nope_width + rotary_width)


def block_partials(query_rows, rope_rows, latent, rotary, lengths, offset, score_scale):
    blocks = latent.shape[1]
    block_width = latent.shape[2]
    scores = score_scale * (
        jnp.einsum("srk,sbpk->bsrp", query_rows, latent, preferred_element_type=jnp.float32)
        + jnp.einsum("srd,sdbp->bsrp", rope_rows, rotary, preferred_element_type=jnp.float32)
    )
    position = (
        offset
        + jnp.arange(blocks, dtype=jnp.int32)[:, None] * block_width
        + jnp.arange(block_width, dtype=jnp.int32)[None, :]
    )
    is_live = position[:, None, None, :] < lengths[None, :, None, None]
    masked = jnp.where(is_live, scores, -1e30)
    block_max = jnp.max(masked, axis=-1)
    weights = jnp.where(is_live, jnp.exp(masked - block_max[..., None]), 0.0)
    block_total = jnp.sum(weights, axis=-1)
    summed = jnp.einsum(
        "bsrp,sbpk->bsrk", weights.astype(jnp.bfloat16), latent, preferred_element_type=jnp.float32
    )
    block_out = (summed / jnp.maximum(block_total, 1.0)[..., None]).astype(jnp.bfloat16)
    return (block_max, block_total, block_out)


def combine(
    block_max,
    block_total,
    block_out,
    absorbed,
    rotary_query,
    fresh_latent,
    fresh_rotary,
    score_scale,
):
    new_scores = score_scale * (
        jnp.einsum("sthk,snk->sthn", absorbed, fresh_latent, preferred_element_type=jnp.float32)
        + jnp.einsum(
            "sthd,snd->sthn", rotary_query, fresh_rotary, preferred_element_type=jnp.float32
        )
    )
    decoding_step_count = fresh_latent.shape[1]
    causal = (jnp.arange(decoding_step_count)[:, None] >= jnp.arange(decoding_step_count)[None, :])[
        None, :, None, :
    ]
    new_masked = jnp.where(causal, new_scores, -1e30)
    row_top = jnp.maximum(jnp.max(block_max, axis=0), jnp.max(new_masked, axis=-1))
    block_weight = block_total * jnp.exp(block_max - row_top[None])
    new_weight = jnp.where(causal, jnp.exp(new_masked - row_top[..., None]), 0.0)
    numerator = jnp.sum(block_weight[..., None] * block_out, axis=0)
    numerator = numerator + jnp.einsum(
        "sthn,snk->sthk", new_weight, fresh_latent.astype(jnp.float32)
    )
    denominator = jnp.sum(block_weight, axis=0) + jnp.sum(new_weight, axis=-1)
    return (numerator / denominator[..., None]).astype(jnp.bfloat16)


def spread_attend(absorbed, rotary_query, key_sets, fresh_latent, fresh_rotary, score_scale):
    slot_count = absorbed.shape[0]
    decoding_step_count = absorbed.shape[1]
    latent_width = absorbed.shape[3]
    all_absorbed, all_rotary = (
        lax.all_gather(absorbed, "dev", axis=2, tiled=True),
        lax.all_gather(rotary_query, "dev", axis=2, tiled=True),
    )
    heads_all = all_absorbed.shape[2]
    query_rows = all_absorbed.reshape(slot_count, decoding_step_count * heads_all, latent_width)
    rope_rows = all_rotary.reshape(slot_count, decoding_step_count * heads_all, all_rotary.shape[3])
    offset = lax.axis_index("dev") * key_sets[0][0].shape[1]
    latent = jnp.concatenate([member[0] for member in key_sets], axis=0)[:, None]
    rotary = jnp.concatenate([member[1] for member in key_sets], axis=0)[:, :, None]
    lengths = jnp.concatenate([member[2] for member in key_sets], axis=0)
    block_max, block_total, block_out = block_partials(
        query_rows, rope_rows, latent, rotary, lengths, offset, score_scale
    )
    stat_shape = (1, slot_count, decoding_step_count, heads_all)
    merged_output = lax.all_to_all(
        block_out.reshape(stat_shape + (latent_width,)),
        "dev",
        split_axis=3,
        concat_axis=0,
        tiled=True,
    )
    mixed_max, mixed_total = (
        lax.all_to_all(
            block_max.reshape(stat_shape), "dev", split_axis=3, concat_axis=0, tiled=True
        ),
        lax.all_to_all(
            block_total.reshape(stat_shape), "dev", split_axis=3, concat_axis=0, tiled=True
        ),
    )
    return combine(
        mixed_max,
        mixed_total,
        merged_output,
        absorbed,
        rotary_query,
        fresh_latent,
        fresh_rotary,
        score_scale,
    )


def body(
    prompt_latent_cache,
    prompt_rope,
    prompt_length,
    dest_slot,
    resident_latent,
    resident_rope,
    resident_length,
    new_latent,
    new_rope,
    query_nope,
    query_rope,
    key_up,
    value_up_weight,
):
    score_scale = attend_scale(query_nope.shape[-1], query_rope.shape[-1])
    resident_count = resident_length.shape[1]
    capacity = query_nope.shape[0] - resident_count
    groups = lax.axis_size("grp")
    destination = dest_slot[0]
    target_group = destination // capacity
    target_slot = destination % capacity
    routing = target_group[None, :] == jnp.arange(groups, dtype=jnp.int32)[:, None]
    route_weight = routing.astype(jnp.bfloat16)
    send_latent = jnp.einsum(
        "gr,rpk->gpk", route_weight, prompt_latent_cache, preferred_element_type=jnp.float32
    ).astype(jnp.bfloat16)
    send_rope = jnp.einsum(
        "gr,rdp->gdp", route_weight, prompt_rope, preferred_element_type=jnp.float32
    ).astype(jnp.bfloat16)
    send_slot = jnp.sum(jnp.where(routing, target_slot[None, :] + 1, 0), axis=1) - 1
    send_length = jnp.sum(jnp.where(routing, prompt_length[0][None, :], 0), axis=1)
    got_latent, got_rope, got_slot, got_length = (
        lax.all_to_all(send_latent, "grp", split_axis=0, concat_axis=0, tiled=True),
        lax.all_to_all(send_rope, "grp", split_axis=0, concat_axis=0, tiled=True),
        lax.all_to_all(send_slot, "grp", split_axis=0, concat_axis=0, tiled=True),
        lax.all_to_all(send_length, "grp", split_axis=0, concat_axis=0, tiled=True),
    )
    placing = got_slot[None, :] == jnp.arange(capacity, dtype=jnp.int32)[:, None]
    place_weight = placing.astype(jnp.bfloat16)
    incoming_latent = jnp.einsum(
        "cs,spk->cpk", place_weight, got_latent, preferred_element_type=jnp.float32
    ).astype(jnp.bfloat16)
    incoming_rope = jnp.einsum(
        "cs,sdp->cdp", place_weight, got_rope, preferred_element_type=jnp.float32
    ).astype(jnp.bfloat16)
    incoming_length = jnp.sum(jnp.where(placing, got_length[None, :], 0), axis=1)
    absorbed = jnp.einsum(
        "sthn,hnk->sthk", query_nope, key_up, preferred_element_type=jnp.float32
    ).astype(jnp.bfloat16)
    attention_result = spread_attend(
        absorbed,
        query_rope,
        [
            (resident_latent, resident_rope, resident_length[0]),
            (incoming_latent, incoming_rope, incoming_length),
        ],
        new_latent,
        new_rope,
        score_scale,
    )
    per_head_output = jnp.einsum(
        "almq,mqb->almb", attention_result, value_up_weight, preferred_element_type=jnp.float32
    )
    return per_head_output.astype(jnp.bfloat16)


def solution(mesh):
    placed = (
        P("grp", "dev", None),
        P("grp", None, "dev"),
        P("grp", None),
        P("grp", None),
        P("grp", "dev", None),
        P("grp", None, "dev"),
        P("grp", None),
        P("grp", None, None),
        P("grp", None, None),
        P("grp", None, "dev", None),
        P("grp", None, "dev", None),
        P("dev", None, None),
        P("dev", None, None),
    )
    return jax.shard_map(
        body, mesh=mesh, in_specs=placed, out_specs=P("grp", None, "dev", None), check_vma=False
    )
```

profile of v0, /device:TPU:6, one launch (start us, length us, event | category | flops | bytes accessed | tf_op | source)
XLA Modules:
  0.0 340.9 jit_solution(5991404762160278673)
XLA Ops:
  6.5 0.8 fusion.46
  7.3 0.7 select_reduce_fusion.1
  8.0 0.7 copy.77
  8.7 10.2 %all-to-all-start = ((s32[32,1,1]{2,1,0:T(1,128)}), s32[32,1,1]{2,1,0:T(1,128)S(1)}, u32[]{:S(2)}, u32[]{:S(2)}) async-start(s32[32,1,1]{2,1,0:T(1,128)} %copy.77), calls=%async_computation | async-start | bytes 32768 | tf_op jit(solution)/shard_map/all_to_all | solution.py:150
  19.0 0.7 copy.78
  19.7 7.1 %all-to-all-done = s32[32,1,1]{2,1,0:T(1,128)S(1)} async-done(((s32[32,1,1]{2,1,0:T(1,128)}), s32[32,1,1]{2,1,0:T(1,128)S(1)}, u32[]{:S(2)}, u32[]{:S(2)}) %all-to-all-start) | async-done | bytes 160 | tf_op jit(solution)/shard_map/all_to_all | solution.py:150
  26.8 5.7 %all-to-all-start.1 = ((s32[32,1,1]{2,1,0:T(1,128)}), s32[32,1,1]{2,1,0:T(1,128)S(1)}, u32[]{:S(2)}, u32[]{:S(2)}) async-start(s32[32,1,1]{2,1,0:T(1,128)} %copy.78), calls=%async_computation.1 | async-start | bytes 32768 | tf_op jit(solution)/shard_map/all_to_all | solution.py:151
  32.6 1.4 convolution_convert_fusion.1
  34.0 0.0 copy-start.4
  34.0 1.6 copy.87
  35.6 4.9 %all-to-all-done.1 = s32[32,1,1]{2,1,0:T(1,128)S(1)} async-done(((s32[32,1,1]{2,1,0:T(1,128)}), s32[32,1,1]{2,1,0:T(1,128)S(1)}, u32[]{:S(2)}, u32[]{:S(2)}) %all-to-all-start.1) | async-done | bytes 160 | tf_op jit(solution)/shard_map/all_to_all | solution.py:151
  40.4 5.9 %all-to-all-start.3 = ((bf16[32,64,256]{2,1,0:T(8,128)(2,1)}), bf16[32,64,256]{2,1,0:T(8,128)(2,1)S(1)}, u32[]{:S(2)}, u32[]{:S(2)}) async-start(bf16[32,64,256]{2,1,0:T(8,128)(2,1)} %copy.87), calls=%async_computation.3 | async-start | bytes 2097152 | tf_op jit(solution)/shard_map/all_to_all | solution.py:149
  46.3 4.8 %convolution_convert_fusion = bf16[32,256,512]{2,0,1:T(8,128)(2,1)} fusion(bf16[2,256,512]{2,1,0:T(8,128)(2,1)S(1)} %copy-done.4, s32[2]{0:T(128)S(1)} %get-tuple-element.10), kind=kOutput, calls=%fused_computation.2 | convolution fusion | flops 20971584 | bytes 8912904 | tf_op jit(solution)/shard_map/gr,rpk->gpk/dot_general | solution.py:139
  51.1 11.3 %copy.80 = bf16[32,256,512]{2,1,0:T(8,128)(2,1)} copy(bf16[32,256,512]{2,0,1:T(8,128)(2,1)} %convolution_convert_fusion) | data formatting | bytes 16777216 | tf_op jit(solution)/shard_map/convert_element_type | solution.py:141
  62.5 7.9 %all-to-all-done.3 = bf16[32,64,256]{2,1,0:T(8,128)(2,1)S(1)} async-done(((bf16[32,64,256]{2,1,0:T(8,128)(2,1)}), bf16[32,64,256]{2,1,0:T(8,128)(2,1)S(1)}, u32[]{:S(2)}, u32[]{:S(2)}) %all-to-all-start.3) | async-done | bytes 1048608 | tf_op jit(solution)/shard_map/all_to_all | solution.py:149
  70.4 7.3 %all-to-all-start.2 = ((bf16[32,256,512]{2,1,0:T(8,128)(2,1)}), bf16[32,256,512]{2,1,0:T(8,128)(2,1)}, u32[]{:S(2)}, u32[]{:S(2)}) async-start(bf16[32,256,512]{2,1,0:T(8,128)(2,1)} %copy.80), calls=%async_computation.2 | async-start | bytes 16777216 | tf_op jit(solution)/shard_map/all_to_all | solution.py:148
  77.7 0.0 copy-start.7
  77.7 0.0 copy-start.9
  77.8 0.0 copy-start.12
  77.8 0.0 all-gather.2.cloned.1.call-start
  77.8 0.9 fusion.12
  78.7 0.0 all-gather.2.cloned.1.call-update
  78.8 0.5 copy.82
  79.3 0.1 copy.89
  79.4 24.0 %all_gather.7 = bf16[4,2,128,64]{3,2,1,0:T(8,128)(2,1)S(1)} all-gather(bf16[4,2,8,64]{3,2,1,0:T(8,128)(2,1)S(1)} %copy-done.9), channel_id=1, replica_groups=mesh['grp'=32,'dev'=16] {'dev'}, dimensions={2}, use_global_device_ids=true | all-gather | bytes 139264 | tf_op jit(solution)/shard_map/all_gather | solution.py:75
  103.4 0.7 reduce.3
  104.1 0.7 reduce.4
  104.8 0.1 select_reduce_fusion
  104.9 0.1 pad_add_fusion
  105.0 0.1 broadcast_compare_fusion
  105.1 21.8 %all-gather.2.cloned.1.call-done = bf16[4,2,128,512]{3,0,1,2:T(4,128)(2,1)} async-done(((bf16[4,2,8,512]{3,0,1,2:T(4,128)(2,1)}), bf16[4,2,128,512]{3,0,1,2:T(4,128)(2,1)}) %all-gather.2.cloned.1.call-update) | async-done | bytes 1048592 | tf_op jit(solution)/shard_map/all_gather | solution.py:74
  126.8 2.5 copy.84
  129.4 0.7 convolution_convert_fusion.2
  130.0 0.1 pad_maximum_fusion.1
  130.2 1.4 fusion.29
  131.5 125.8 %all-to-all-done.2 = bf16[32,256,512]{2,1,0:T(8,128)(2,1)} async-done(((bf16[32,256,512]{2,1,0:T(8,128)(2,1)}), bf16[32,256,512]{2,1,0:T(8,128)(2,1)}, u32[]{:S(2)}, u32[]{:S(2)}) %all-to-all-start.2) | async-done | bytes 8388640 | tf_op jit(solution)/shard_map/all_to_all | solution.py:148
  257.4 8.2 %fusion.5 = bf16[2,256,512]{2,0,1:T(2,128)(2,1)S(1)} fusion(bf16[32,256,512]{2,1,0:T(8,128)(2,1)} %all-to-all-done.2, s32[32]{0:T(128)S(1)} %reduce.3), kind=kOutput, calls=%fused_computation.10 | convolution fusion | flops 17039424 | bytes 8913024 | tf_op jit(solution)/shard_map/cs,spk->cpk/dot_general | solution.py:155
  265.6 1.1 pad_maximum_fusion
  266.7 0.1 copy-done.1
  266.8 0.3 copy-done.2
  267.1 0.8 fusion.57
  267.9 0.2 fusion.22
  268.1 0.8 copy.92
  268.9 10.4 %all-to-all-start.4 = ((f32[1,4,2,128]{1,2,0,3:T(2,128)}), f32[1,4,2,128]{1,2,0,3:T(2,128)S(1)}, u32[]{:S(2)}, u32[]{:S(2)}) async-start(f32[1,4,2,128]{1,2,0,3:T(2,128)} %copy.92), calls=%async_computation.4 | async-start | bytes 262144 | tf_op jit(solution)/shard_map/all_to_all | solution.py:99
  279.3 0.8 copy.94
  280.1 7.9 %all-to-all-done.4 = f32[1,4,2,128]{1,2,0,3:T(2,128)S(1)} async-done(((f32[1,4,2,128]{1,2,0,3:T(2,128)}), f32[1,4,2,128]{1,2,0,3:T(2,128)S(1)}, u32[]{:S(2)}, u32[]{:S(2)}) %all-to-all-start.4) | async-done | bytes 4128 | tf_op jit(solution)/shard_map/all_to_all | solution.py:99
  288.1 3.5 %all-to-all-start.5 = ((f32[1,4,2,128]{1,2,0,3:T(2,128)}), f32[1,4,2,128]{1,2,0,3:T(2,128)S(1)}, u32[]{:S(2)}, u32[]{:S(2)}) async-start(f32[1,4,2,128]{1,2,0,3:T(2,128)} %copy.94), calls=%async_computation.5 | async-start | bytes 262144 | tf_op jit(solution)/shard_map/all_to_all | solution.py:96
  291.6 0.9 divide_convert_fusion
  292.5 0.0 copy-start.10
  292.5 0.0 copy-start.11
  292.5 2.1 copy.99
  294.6 5.7 %all-to-all-done.5 = f32[1,4,2,128]{1,2,0,3:T(2,128)S(1)} async-done(((f32[1,4,2,128]{1,2,0,3:T(2,128)}), f32[1,4,2,128]{1,2,0,3:T(2,128)S(1)}, u32[]{:S(2)}, u32[]{:S(2)}) %all-to-all-start.5) | async-done | bytes 4128 | tf_op jit(solution)/shard_map/all_to_all | solution.py:96
  300.3 3.9 %all-to-all-start.6 = ((bf16[1,4,2,128,512]{4,2,1,0,3:T(2,128)(2,1)}), bf16[1,4,2,128,512]{4,2,1,0,3:T(2,128)(2,1)S(1)}, u32[]{:S(2)}, u32[]{:S(2)}) async-start(bf16[1,4,2,128,512]{4,2,1,0,3:T(2,128)(2,1)} %copy.99), calls=%async_computation.6 | async-start | bytes 2097152 | tf_op jit(solution)/shard_map/all_to_all | solution.py:88
  304.2 0.3 fusion.34
  304.4 0.2 fusion.58
  304.7 0.3 copy.109
  304.9 0.3 copy.110
  305.3 0.1 fusion.52
  305.5 25.1 %all-to-all-done.6 = bf16[1,4,2,128,512]{4,2,1,0,3:T(2,128)(2,1)S(1)} async-done(((bf16[1,4,2,128,512]{4,2,1,0,3:T(2,128)(2,1)}), bf16[1,4,2,128,512]{4,2,1,0,3:T(2,128)(2,1)S(1)}, u32[]{:S(2)}, u32[]{:S(2)}) %all-to-all-start.6) | async-done | bytes 1048608 | tf_op jit(solution)/shard_map/all_to_all | solution.py:88
  330.5 1.1 convert.3
  331.7 1.1 fusion.2
  332.9 0.3 fusion.11
  333.1 0.3 fusion.13
  333.4 0.6 copy.102
  (26 shorter events, 0.1 us)
Async XLA Ops:
  6.5 71.3 %copy-start = (bf16[8,128,512]{2,1,0:T(8,128)(2,1)S(1)}, bf16[8,128,512]{2,1,0:T(8,128)(2,1)}, u32[]{:S(2)}) copy-start(bf16[8,128,512]{2,1,0:T(8,128)(2,1)} %param.24) | copy-start | bytes 3145732
  8.7 18.1 %all-to-all-start = ((s32[32,1,1]{2,1,0:T(1,128)}), s32[32,1,1]{2,1,0:T(1,128)S(1)}, u32[]{:S(2)}, u32[]{:S(2)}) async-start(s32[32,1,1]{2,1,0:T(1,128)} %copy.77), calls=%async_computation | async-start | bytes 32768 | tf_op jit(solution)/shard_map/all_to_all | solution.py:150
  26.8 13.6 %all-to-all-start.1 = ((s32[32,1,1]{2,1,0:T(1,128)}), s32[32,1,1]{2,1,0:T(1,128)S(1)}, u32[]{:S(2)}, u32[]{:S(2)}) async-start(s32[32,1,1]{2,1,0:T(1,128)} %copy.78), calls=%async_computation.1 | async-start | bytes 32768 | tf_op jit(solution)/shard_map/all_to_all | solution.py:151
  34.0 12.3 %copy-start.4 = (bf16[2,256,512]{2,1,0:T(8,128)(2,1)S(1)}, bf16[2,256,512]{2,1,0:T(8,128)(2,1)}, u32[]{:S(2)}) copy-start(bf16[2,256,512]{2,1,0:T(8,128)(2,1)} %param.13) | copy-start | bytes 1572868
  40.4 30.0 %all-to-all-start.3 = ((bf16[32,64,256]{2,1,0:T(8,128)(2,1)}), bf16[32,64,256]{2,1,0:T(8,128)(2,1)S(1)}, u32[]{:S(2)}, u32[]{:S(2)}) async-start(bf16[32,64,256]{2,1,0:T(8,128)(2,1)} %copy.87), calls=%async_computation.3 | async-start | bytes 2097152 | tf_op jit(solution)/shard_map/all_to_all | solution.py:149
  62.5 15.4 %copy-start.8 = (bf16[4,2,8,128]{3,2,1,0:T(8,128)(2,1)S(1)}, bf16[4,2,8,128]{3,2,1,0:T(8,128)(2,1)}, u32[]{:S(2)}) copy-start(bf16[4,2,8,128]{3,2,1,0:T(8,128)(2,1)} %param.22) | copy-start | bytes 49156
  62.5 16.3 %copy-start.5 = (bf16[2,256,512]{2,1,0:T(8,128)(2,1)S(1)}, bf16[2,256,512]{2,1,0:T(8,128)(2,1)}, u32[]{:S(2)}) copy-start(bf16[2,256,512]{2,1,0:T(8,128)(2,1)} %param.17) | copy-start | bytes 1572868
  70.4 187.0 %all-to-all-start.2 = ((bf16[32,256,512]{2,1,0:T(8,128)(2,1)}), bf16[32,256,512]{2,1,0:T(8,128)(2,1)}, u32[]{:S(2)}, u32[]{:S(2)}) async-start(bf16[32,256,512]{2,1,0:T(8,128)(2,1)} %copy.80), calls=%async_computation.2 | async-start | bytes 16777216 | tf_op jit(solution)/shard_map/all_to_all | solution.py:148
  77.7 1.6 copy-start.7
  77.7 1.6 copy-start.9
  77.8 27.1 %copy-start.12 = (s32[1,2]{1,0:T(1,128)S(1)}, s32[1,2]{1,0:T(1,128)}, u32[]{:S(2)}) copy-start(s32[1,2]{1,0:T(1,128)} %param.19) | copy-start | bytes 28
  77.8 49.1 %all-gather.2.cloned.1.call-start = ((), (), s32[]{:S(2)}) async-start(), calls=%async_computation.7 | async-start | bytes 1114112 | tf_op jit(solution)/shard_map/all_gather | solution.py:74
  265.5 1.2 copy-start.1
  265.6 1.5 copy-start.2
  268.9 19.2 %all-to-all-start.4 = ((f32[1,4,2,128]{1,2,0,3:T(2,128)}), f32[1,4,2,128]{1,2,0,3:T(2,128)S(1)}, u32[]{:S(2)}, u32[]{:S(2)}) async-start(f32[1,4,2,128]{1,2,0,3:T(2,128)} %copy.92), calls=%async_computation.4 | async-start | bytes 262144 | tf_op jit(solution)/shard_map/all_to_all | solution.py:99
  288.1 12.2 %all-to-all-start.5 = ((f32[1,4,2,128]{1,2,0,3:T(2,128)}), f32[1,4,2,128]{1,2,0,3:T(2,128)S(1)}, u32[]{:S(2)}, u32[]{:S(2)}) async-start(f32[1,4,2,128]{1,2,0,3:T(2,128)} %copy.94), calls=%async_computation.5 | async-start | bytes 262144 | tf_op jit(solution)/shard_map/all_to_all | solution.py:96
  292.5 11.7 %copy-start.6 = (bf16[4,2,8,512]{3,0,1,2:T(4,128)(2,1)S(1)}, bf16[4,2,8,512]{3,0,1,2:T(4,128)(2,1)}, u32[]{:S(2)}) copy-start(bf16[4,2,8,512]{3,0,1,2:T(4,128)(2,1)} %fusion.12) | copy-start | bytes 196612
  292.5 11.7 %copy-start.10 = (bf16[4,2,512]{2,1,0:T(2,128)(2,1)S(1)}, bf16[4,2,512]{2,1,0:T(2,128)(2,1)}, u32[]{:S(2)}) copy-start(bf16[4,2,512]{2,1,0:T(2,128)(2,1)} %param.20) | copy-start | bytes 24580
  292.5 12.0 %copy-start.11 = (bf16[4,2,64]{2,1,0:T(2,128)(2,1)S(1)}, bf16[4,2,64]{2,1,0:T(2,128)(2,1)}, u32[]{:S(2)}) copy-start(bf16[4,2,64]{2,1,0:T(2,128)(2,1)} %param.21) | copy-start | bytes 3076
  300.3 30.3 %all-to-all-start.6 = ((bf16[1,4,2,128,512]{4,2,1,0,3:T(2,128)(2,1)}), bf16[1,4,2,128,512]{4,2,1,0,3:T(2,128)(2,1)S(1)}, u32[]{:S(2)}, u32[]{:S(2)}) async-start(bf16[1,4,2,128,512]{4,2,1,0,3:T(2,128)(2,1)} %copy.99), calls=%async_computation.6 | async-start | bytes 2097152 | tf_op jit(solution)/shard_map/all_to_all | solution.py:88
  331.7 1.4 copy-start.3
Sparse Core Ops, SparseCore 0:
  80.7 46.0 all-gather.1
where the time goes:
time: 347 us; the launch traced here: 341 us
  waiting for transfers between devices  206 us (59%)
  starting transfers between devices  47 us (14%)
  blocking collectives  24 us (7%)
  local copies, waits for them, and re-layouts  22.8 us (7%)
  matrix products  20 us (6%)
  between operations  13.7 us (4%)
  other arithmetic  7.02 us (2%)
    all_to_all x1, waiting for transfers between devices, body(): lax.all_to_all(send_latent, 'grp', split_axis=0, concat_axis=0, tiled=True)  126 us
    all_to_all x1, waiting for transfers between devices, spread_attend(): lax.all_to_all(block_out.reshape(stat_shape + (latent_width,)), 'dev', sp...  25.1 us
    all_gather x1, blocking collectives, spread_attend(): lax.all_gather(rotary_query, 'dev', axis=2, tiled=True)  24 us
    all_gather x1, waiting for transfers between devices, spread_attend(): lax.all_gather(absorbed, 'dev', axis=2, tiled=True)  21.8 us
    convert_element_type x1, local copies, waits for them, and re-layouts, body(): send_latent = jnp.einsum('gr,rpk->gpk', route_weight, prompt_latent_cache...  11.3 us
    all_to_all x1, starting transfers between devices, spread_attend(): lax.all_to_all(block_total.reshape(stat_shape), 'dev', split_axis=3, conc...  10.4 us
    all_to_all x1, starting transfers between devices, body(): lax.all_to_all(send_slot, 'grp', split_axis=0, concat_axis=0, tiled=True)  10.2 us
    dot_general x1, matrix products, body(): jnp.einsum('cs,spk->cpk', place_weight, got_latent, preferred_element_typ...  8.18 us
  transfers between devices with their start and end apart: 8, of which 8 were waited for; matrix products, arithmetic and copies ran while one was open for 10% of the time, Pallas kernels for 0%

commit v1 on v0

v1 whole, which is shorter than its diff:
```python
import functools
import math

import jax
import jax.numpy as jnp
from jax import lax
from jax.experimental import pallas as pl
from jax.experimental.pallas import tpu as pltpu
from jax.sharding import PartitionSpec as P

MESH = pl.DeviceIdType.MESH
F32 = jnp.float32
BF16 = jnp.bfloat16
NX, NY, NZ = 4, 8, 8
NG = NX * NY
NEG = -1e30


def attend_scale(nope_width, rotary_width):
    return (0.1 * math.log(40.0) + 1.0) ** 2 / math.sqrt(nope_width + rotary_width)


def iota(shape, axis):
    return lax.broadcasted_iota(jnp.int32, shape, axis)


def columns_of(rows, field):
    n = rows.shape[0]
    hit = iota((n, 16, 128), 2) == iota((n, 16, 128), 1) + 16 * field
    return jnp.sum(jnp.where(hit, jnp.broadcast_to(rows, (n, 16, 128)), 0.0), axis=-1, keepdims=True)


def rows_of(fields):
    n = fields[0].shape[0]
    lane, sub = iota((n, 16, 128), 2), iota((n, 16, 128), 1)
    packed = jnp.zeros((n, 16, 128), F32)
    for f, column in enumerate(fields):
        packed = jnp.where(lane == sub + 16 * f, jnp.broadcast_to(column, (n, 16, 128)), packed)
    return jnp.sum(packed, axis=1, keepdims=True)


def absorb(q32, kup):
    head = iota((32, 512), 0) % 8
    total = jnp.zeros((32, 512), F32)
    for h in range(8):
        total = jnp.where(head == h, jnp.dot(q32, kup[h], preferred_element_type=F32), total)
    return total.astype(BF16)


def new_scores(scale, absorbed, ropes, fresh, fresh_rope):
    step = iota((16, 1), 0) // 8
    out = []
    for s in range(2):
        q = absorbed[s * 16 : (s + 1) * 16].astype(F32)
        pair = []
        for n in range(2):
            v = jnp.sum(q * fresh[s][n], axis=-1, keepdims=True)
            v = v + jnp.sum(ropes[s] * fresh_rope[s][n], axis=-1, keepdims=True)
            v = v * scale
            pair.append(v if n == 0 else jnp.where(step >= 1, v, NEG))
        out.append(pair)
    return out


def attend(scale, gathered, latent, rope, lengths, offset, out_bf, out_st):
    ropes = gathered[:, 128:144, :].reshape(256, 128)
    position = offset + iota((256, 256), 1)
    blank = jnp.zeros((64, 256), BF16)
    fields = [None] * 4
    for s in range(2):
        q = jnp.concatenate(
            [gathered[:, k * 32 + s * 16 : k * 32 + s * 16 + 16, :].reshape(256, 128) for k in range(4)],
            axis=1,
        )
        keys = latent[s]
        rk = jnp.concatenate([rope[s], blank] if s == 0 else [blank, rope[s]], axis=0)
        scores = lax.dot_general(q, keys, (((1,), (1,)), ((), ())), preferred_element_type=F32)
        scores = scale * (scores + jnp.dot(ropes, rk, preferred_element_type=F32))
        live = position < lengths[s]
        scores = jnp.where(live, scores, NEG)
        top = jnp.max(scores, axis=-1, keepdims=True)
        weights = jnp.where(live, jnp.exp(scores - top), 0.0)
        total = jnp.sum(weights, axis=-1, keepdims=True)
        summed = jnp.dot(weights.astype(BF16), keys, preferred_element_type=F32)
        summed = summed / jnp.maximum(total, 1.0)
        out_bf[:, s * 16 : (s + 1) * 16, :] = summed.reshape(16, 16, 512).astype(BF16)
        fields[s] = top.reshape(16, 16, 1)
        fields[2 + s] = total.reshape(16, 16, 1)
    out_st[...] = rows_of(fields)


def merge_cores(own_bf, own_st, other_bf, other_st, out_bf, out_st):
    fields = [None] * 4
    for s in range(2):
        m1, l1 = columns_of(own_st, s), columns_of(own_st, 2 + s)
        m2, l2 = columns_of(other_st[...], s), columns_of(other_st[...], 2 + s)
        top = jnp.maximum(m1, m2)
        a, b = l1 * jnp.exp(m1 - top), l2 * jnp.exp(m2 - top)
        total = a + b
        under = 1.0 / jnp.maximum(total, 1.0)
        rows = slice(s * 16, (s + 1) * 16)
        o = own_bf(rows).astype(F32) * (a * under) + other_bf[:, rows, :].astype(F32) * (b * under)
        out_bf[:, rows, :] = o.astype(BF16)
        fields[s], fields[2 + s] = top, total
    out_st[...] = rows_of(fields)


def finish(blocks, stats, fresh_scores, fresh, vup):
    rows = []
    for s in range(2):
        m, l = columns_of(stats[...], s), columns_of(stats[...], 2 + s)
        n0, n1 = fresh_scores[s]
        top = jnp.maximum(jnp.max(m, axis=0), jnp.maximum(n0, n1))
        w = l * jnp.exp(m - top[None])
        w0 = jnp.exp(n0 - top)
        w1 = jnp.where(n1 > NEG, jnp.exp(n1 - top), 0.0)
        under = jnp.sum(w, axis=0) + w0 + w1
        total = w0 * fresh[s][0] + w1 * fresh[s][1]
        for j in range(NZ):
            total = total + w[j] * blocks[j, s * 16 : (s + 1) * 16, :].astype(F32)
        rows.append(total / under)
    attended = jnp.concatenate(rows, axis=0).astype(BF16)
    head = iota((32, 128), 0) % 8
    out = jnp.zeros((32, 128), F32)
    for h in range(8):
        out = jnp.where(head == h, jnp.dot(attended, vup[h], preferred_element_type=F32), out)
    return out


def kernel(
    scale,
    plat_hbm, prope, plen, dest, rlat_hbm, rrope, rlen, nlat, nrope, qn, qr, kup_hbm, vup_hbm,
    out,
    plat, rlat, kup, vup, aux, pay, xsend, xrecv, g_res, g_inc,
    obf, ost, sib_bf, sib_st, zs_bf, zs_st, zr_bf, zr_st, ret_send, ret_recv, small,
    load_sem, aux_ss, aux_rs, y_ss, y_rs, x_ss, x_rs, gz_ss, gz_rs, gs_ss, gs_rs,
    cs_ss, cs_rs, zo_ss, zo_rs, zt_ss, zt_rs, ret_ss, ret_rs,
):
    g, d = lax.axis_index("grp"), lax.axis_index("dev")
    x, y = g // NY, g % NY
    z, c = d // 2, d % 2
    mine = c * NZ + z
    sibling = (g, z * 2 + 1 - c)

    loads = [
        pltpu.make_async_copy(src, dst, load_sem.at[i])
        for i, (src, dst) in enumerate(
            [(kup_hbm, kup), (rlat_hbm, rlat), (plat_hbm, plat), (vup_hbm, vup)]
        )
    ]
    for load in loads:
        load.start()

    barrier = pltpu.get_barrier_semaphore()

    def greet(k, _):
        pl.semaphore_signal(barrier, inc=1, device_id=((g + k) % NG, d), device_id_type=MESH)
        return 0

    lax.fori_loop(1, NG, greet, 0)
    for k in range(1, NZ):
        pl.semaphore_signal(barrier, inc=1, device_id=(g, ((z + k) % NZ) * 2 + c), device_id_type=MESH)
    pl.semaphore_signal(barrier, inc=1, device_id=sibling, device_id_type=MESH)

    def remote(src, dst, ss, rs, device):
        return pltpu.make_async_remote_copy(
            src_ref=src, dst_ref=dst, send_sem=ss, recv_sem=rs, device_id=device, device_id_type=MESH
        )

    qn_all = qn[...].astype(F32).reshape(64, 128)
    qr_all = qr[...].astype(F32).reshape(64, 64)
    fresh_all = nlat[...].astype(F32)
    fresh_rope_all = nrope[...].astype(F32)
    for i in range(2):
        s = 2 + i
        for n in range(2):
            for k in range(4):
                small[n * 4 + k : n * 4 + k + 1, :] = fresh_all[s, n : n + 1, k * 128 : (k + 1) * 128]
        rope_rows = jnp.concatenate(
            [qr_all[s * 16 : s * 16 + 8], qr_all[s * 16 + 8 : s * 16 + 16]], axis=1
        )
        payload = jnp.concatenate([qn_all[s * 16 : (s + 1) * 16], rope_rows, small[...]], axis=0)
        pay[y, i] = payload.astype(BF16)
        aux[g * 2 + i, 0:1, :] = jnp.full((1, 128), dest[0, i].astype(F32))
        aux[g * 2 + i, 1:2, :] = jnp.concatenate(
            [fresh_rope_all[s, 0:1], fresh_rope_all[s, 1:2]], axis=1
        )

    pl.semaphore_wait(barrier, NG - 1 + NZ - 1 + 1)

    def y_copy(to, frm):
        return remote(pay.at[y], pay.at[y], y_ss.at[to], y_rs.at[frm], (x * NY + to, d))

    for k in range(1, NY):
        y_copy((y + k) % NY, y).start()

    def aux_copy(to, frm):
        ref = aux.at[pl.ds(g * 2, 2)]
        return remote(ref, ref, aux_ss.at[to], aux_rs.at[frm], (to, d))

    def send_aux(k, _):
        aux_copy((g + k) % NG, g).start()
        return 0

    lax.fori_loop(1, NG, send_aux, 0)

    def gather_start(p, gathered, absorbed, ropes):
        for k in range(4):
            gathered[mine, k * 32 : (k + 1) * 32, :] = absorbed[:, k * 128 : (k + 1) * 128]
        gathered[mine, 128:144, :] = jnp.concatenate(ropes, axis=1).astype(BF16)
        for k in range(1, NZ):
            to = (z + k) % NZ
            gather_z(p, gathered, to, z).start()
        gather_sib(p, gathered, z).start()

    def gather_z(p, gathered, to, frm):
        ref = gathered.at[mine]
        return remote(ref, ref, gz_ss.at[p, to], gz_rs.at[p, frm], (g, to * 2 + c))

    def gather_sib(p, gathered, frm):
        ref = gathered.at[c * NZ + frm]
        return remote(ref, ref, gs_ss.at[p, frm], gs_rs.at[p, frm], sibling)

    def gather_forward(p, gathered):
        for k in (1, 7, 2, 6, 3, 5, 4):
            frm = (z + k) % NZ
            gather_z(p, gathered, frm, frm).wait_recv()
            gather_sib(p, gathered, frm).start()

    def gather_finish(p, gathered):
        for frm in range(NZ):
            gather_sib(p, gathered, frm).wait_recv()

    loads[0].wait()
    absorbed_res = absorb(qn_all[0:32].astype(BF16), kup)
    ropes_res = [qr_all[0:16], qr_all[16:32]]
    gather_start(0, g_res, absorbed_res, ropes_res)
    fresh_res = [[fresh_all[s, n : n + 1] for n in range(2)] for s in range(2)]
    fresh_rope_res = [[fresh_rope_all[s, n : n + 1] for n in range(2)] for s in range(2)]
    scores_res = new_scores(scale, absorbed_res, ropes_res, fresh_res, fresh_rope_res)

    for k in range(1, NY):
        frm = (y + k) % NY
        y_copy(frm, frm).wait_recv()

    def wait_aux(k, _):
        frm = (g + k) % NG
        aux_copy(frm, frm).wait_recv()
        return 0

    lax.fori_loop(1, NG, wait_aux, 0)

    def x_copy(to, frm):
        return remote(xsend.at[to], xrecv.at[x], x_ss.at[to], x_rs.at[frm], (to * NY + y, d))

    for k in (1, 2, 3, 0):
        to = (x + k) % NX
        for r in range(2):
            wanted = aux[(to * NY + y) * 2 + r, 0:1, :]
            block = jnp.zeros((32, 128), F32)
            for j in range(NY):
                for i in range(2):
                    here = ((x * NY + j) * 2 + i).astype(F32)
                    hit = jnp.broadcast_to(wanted == here, (32, 128))
                    block = jnp.where(hit, pay[j, i].astype(F32), block)
            if k:
                xsend[to, r] = block.astype(BF16)
            else:
                xrecv[x, r] = block.astype(BF16)
        if k:
            x_copy(to, x).start()

    gather_forward(0, g_res)

    for k in range(1, NX):
        frm = (x + k) % NX
        x_copy(frm, frm).wait_recv()
    queries, ropes_inc, fresh_inc, fresh_rope_inc = [], [], [], []
    for r in range(2):
        block = xrecv[0, r].astype(F32)
        for j in range(1, NX):
            block = block + xrecv[j, r].astype(F32)
        queries.append(block[0:16])
        ropes_inc.append(jnp.concatenate([block[16:24, 0:64], block[16:24, 64:128]], axis=0))
        small[...] = block[24:32]
        fresh_inc.append(
            [
                jnp.concatenate([small[n * 4 + k : n * 4 + k + 1, :] for k in range(4)], axis=1)
                for n in range(2)
            ]
        )
        row = aux[dest[0, r], 1:2, :]
        fresh_rope_inc.append([row[:, 0:64], row[:, 64:128]])
    absorbed_inc = absorb(jnp.concatenate(queries, axis=0).astype(BF16), kup)
    gather_start(1, g_inc, absorbed_inc, ropes_inc)
    scores_inc = new_scores(scale, absorbed_inc, ropes_inc, fresh_inc, fresh_rope_inc)

    offset = d * 256

    def cores_copy(p):
        half = pl.ds((1 - c) * NZ, NZ)
        return (
            remote(obf.at[p, half], sib_bf.at[p], cs_ss.at[p, 0], cs_rs.at[p, 0], sibling),
            remote(ost.at[p, half], sib_st.at[p], cs_ss.at[p, 1], cs_rs.at[p, 1], sibling),
        )

    def out_copy(p, to, frm):
        device = (g, to * 2 + c)
        return (
            remote(zs_bf.at[p, to], zr_bf.at[p, z], zo_ss.at[p, to], zo_rs.at[p, frm], device),
            remote(zs_st.at[p, to], zr_st.at[p, z], zt_ss.at[p, to], zt_rs.at[p, frm], device),
        )

    def partials(p, gathered, latent, rope, lengths):
        attend(scale, gathered, latent, rope, lengths, offset, obf.at[p], ost.at[p])
        for copy in cores_copy(p):
            copy.start()

    def exchange(p):
        for copy in cores_copy(p):
            copy.wait_recv()
        own = pl.ds(c * NZ, NZ)
        merge_cores(
            lambda rows: obf[p, own, rows, :], ost[p, own], sib_bf.at[p], sib_st.at[p],
            zs_bf.at[p], zs_st.at[p],
        )
        for k in (4, 3, 5, 2, 6, 1, 7):
            for copy in out_copy(p, (z + k) % NZ, z):
                copy.start()
        zr_bf[p, z] = zs_bf[p, z]
        zr_st[p, z] = zs_st[p, z]

    def collect(p):
        for k in range(1, NZ):
            frm = (z + k) % NZ
            for copy in out_copy(p, frm, frm):
                copy.wait_recv()

    gather_finish(0, g_res)
    loads[1].wait()
    partials(0, g_res, rlat, rrope, [rlen[0, 0], rlen[0, 1]])
    gather_forward(1, g_inc)
    exchange(0)
    gather_finish(1, g_inc)
    loads[2].wait()
    partials(1, g_inc, plat, prope, [plen[0, 0], plen[0, 1]])
    exchange(1)

    loads[3].wait()
    collect(0)
    out_res = finish(zr_bf.at[0], zr_st.at[0], scores_res, fresh_res, vup)
    out[0:2] = out_res.reshape(2, 2, 8, 128).astype(BF16)

    collect(1)
    out_inc = finish(zr_bf.at[1], zr_st.at[1], scores_inc, fresh_inc, vup)

    def ret_block(to):
        block = jnp.zeros((16, 128), F32)
        for r in range(2):
            goal = aux[g * 2 + r, 0:1, :]
            first = (to * 2).astype(F32)
            hit = (goal == first) | (goal == first + 1.0)
            block = jnp.where(jnp.broadcast_to(hit, (16, 128)), out_inc[r * 16 : (r + 1) * 16], block)
        return block.astype(BF16)

    def ret_copy(to, frm):
        return remote(ret_send.at[to], ret_recv.at[g], ret_ss.at[to], ret_rs.at[frm], (to, d))

    def ret_start(k, _):
        to = (g + k) % NG
        ret_send[to] = ret_block(to)
        ret_copy(to, g).start()
        return 0

    lax.fori_loop(1, NG, ret_start, 0)
    ret_recv[g] = ret_block(g)

    def ret_wait(k, _):
        frm = (g + k) % NG
        ret_copy(frm, frm).wait_recv()
        return 0

    lax.fori_loop(1, NG, ret_wait, 0)

    def choose(frm, chosen):
        block = ret_recv[frm].astype(F32)
        picked = []
        for i in range(2):
            here = (g * 2 + i).astype(F32)
            hit = (aux[frm * 2, 0:1, :] == here) | (aux[frm * 2 + 1, 0:1, :] == here)
            picked.append(jnp.where(jnp.broadcast_to(hit, (16, 128)), block, chosen[i]))
        return tuple(picked)

    zero = jnp.zeros((16, 128), F32)
    chosen = lax.fori_loop(0, NG, choose, (zero, zero))
    for i in range(2):
        out[2 + i] = chosen[i].reshape(2, 8, 128).astype(BF16)

    def drain(k, _):
        to = (g + k) % NG
        aux_copy(to, g).wait_send()
        ret_copy(to, g).wait_send()
        return 0

    lax.fori_loop(1, NG, drain, 0)
    for k in range(1, NY):
        y_copy((y + k) % NY, y).wait_send()
    for k in range(1, NX):
        x_copy((x + k) % NX, x).wait_send()
    for p, gathered in ((0, g_res), (1, g_inc)):
        for k in range(1, NZ):
            to = (z + k) % NZ
            gather_z(p, gathered, to, z).wait_send()
            for copy in out_copy(p, to, z):
                copy.wait_send()
        for frm in range(NZ):
            gather_sib(p, gathered, frm).wait_send()
        for copy in cores_copy(p):
            copy.wait_send()


def body(
    prompt_latent_cache, prompt_rope, prompt_length, dest_slot, resident_latent, resident_rope,
    resident_length, new_latent, new_rope, query_nope, query_rope, key_up, value_up_weight,
):
    scale = attend_scale(query_nope.shape[-1], query_rope.shape[-1])
    vmem = pl.BlockSpec(memory_space=pltpu.VMEM)
    smem = pl.BlockSpec(memory_space=pltpu.SMEM)
    hbm = pl.BlockSpec(memory_space=pl.ANY)
    dma = pltpu.SemaphoreType.DMA
    return pl.pallas_call(
        functools.partial(kernel, scale),
        out_shape=jax.ShapeDtypeStruct((4, 2, 8, 128), BF16),
        in_specs=[hbm, vmem, smem, smem, hbm, vmem, smem, vmem, vmem, vmem, vmem, hbm, hbm],
        out_specs=vmem,
        scratch_shapes=[
            pltpu.VMEM((2, 256, 512), BF16),
            pltpu.VMEM((2, 256, 512), BF16),
            pltpu.VMEM((8, 128, 512), BF16),
            pltpu.VMEM((8, 512, 128), BF16),
            pltpu.VMEM((NG * 2, 2, 128), F32),
            pltpu.VMEM((NY, 2, 32, 128), BF16),
            pltpu.VMEM((NX, 2, 32, 128), BF16),
            pltpu.VMEM((NX, 2, 32, 128), BF16),
            pltpu.VMEM((16, 144, 128), BF16),
            pltpu.VMEM((16, 144, 128), BF16),
            pltpu.VMEM((2, 16, 32, 512), BF16),
            pltpu.VMEM((2, 16, 1, 128), F32),
            pltpu.VMEM((2, NZ, 32, 512), BF16),
            pltpu.VMEM((2, NZ, 1, 128), F32),
            pltpu.VMEM((2, NZ, 32, 512), BF16),
            pltpu.VMEM((2, NZ, 1, 128), F32),
            pltpu.VMEM((2, NZ, 32, 512), BF16),
            pltpu.VMEM((2, NZ, 1, 128), F32),
            pltpu.VMEM((NG, 16, 128), BF16),
            pltpu.VMEM((NG, 16, 128), BF16),
            pltpu.VMEM((8, 128), F32),
            dma((4,)),
            dma((NG,)), dma((NG,)),
            dma((NY,)), dma((NY,)),
            dma((NX,)), dma((NX,)),
            dma((2, NZ)), dma((2, NZ)),
            dma((2, NZ)), dma((2, NZ)),
            dma((2, 2)), dma((2, 2)),
            dma((2, NZ)), dma((2, NZ)),
            dma((2, NZ)), dma((2, NZ)),
            dma((NG,)), dma((NG,)),
        ],
        compiler_params=pltpu.CompilerParams(
            collective_id=0, has_side_effects=True, vmem_limit_bytes=48 << 20
        ),
        name="latent_attend",
    )(
        prompt_latent_cache, prompt_rope, prompt_length, dest_slot, resident_latent, resident_rope,
        resident_length, new_latent, new_rope, query_nope, query_rope, key_up, value_up_weight,
    )


def solution(mesh):
    placed = (
        P("grp", "dev", None),
        P("grp", None, "dev"),
        P("grp", None),
        P("grp", None),
        P("grp", "dev", None),
        P("grp", None, "dev"),
        P("grp", None),
        P("grp", None, None),
        P("grp", None, None),
        P("grp", None, "dev", None),
        P("grp", None, "dev", None),
        P("dev", None, None),
        P("dev", None, None),
    )
    return jax.shard_map(
        body, mesh=mesh, in_specs=placed, out_specs=P("grp", None, "dev", None), check_vma=False
    )
```

time: 347 us -> 70.1 us (0.20); the launches traced: 341 us -> 68.9 us
  waiting for transfers between devices: 206 us -> 0 us
  Pallas kernels: 0 us -> 57.3 us
  starting transfers between devices: 47 us -> 0 us
  blocking collectives: 24 us -> 0 us
  matrix products: 20 us -> 0 us
  between operations: 13.7 us -> 0.02 us
  local copies, waits for them, and re-layouts: 22.8 us -> 11.6 us
  other arithmetic: 7.02 us -> 0 us
    all_to_all x7 -> x0, waiting for transfers between devices: 184 us -> none  [the longest x1 126 us: body(): lax.all_to_all(send_latent, 'grp', split_axis=0, concat_axis=0, tiled=True)]
    pallas_call x0 -> x1, Pallas kernels: none -> 57.3 us  [body(): pl.pallas_call(functools.partial(kernel, scale), out_shape=jax.ShapeDtype...]
    all_to_all x7 -> x0, starting transfers between devices: 47 us -> none  [the longest x1 10.4 us: spread_attend(): lax.all_to_all(block_total.reshape(stat_shape), 'dev', split_axis=3, conc...]
    all_gather x1 -> x0, blocking collectives: 24 us -> none  [spread_attend(): lax.all_gather(rotary_query, 'dev', axis=2, tiled=True)]
    all_gather x1 -> x0, waiting for transfers between devices: 21.8 us -> none  [spread_attend(): lax.all_gather(absorbed, 'dev', axis=2, tiled=True)]
    dot_general x12 -> x0, matrix products: 20 us -> none  [the longest x1 8.18 us: body(): jnp.einsum('cs,spk->cpk', place_weight, got_latent, preferred_element_typ...]
    convert_element_type x3 -> x0, local copies, waits for them, and re-layouts: 13.5 us -> none  [the longest x1 11.3 us: body(): send_latent = jnp.einsum('gr,rpk->gpk', route_weight, prompt_latent_cache...]
    unnamed x28 -> x27, local copies, waits for them, and re-layouts: 1.11 us -> 11.6 us
  transfers between devices with their start and end apart: 8 -> 0, of which waited for: 8 -> 0; matrix products, arithmetic and copies ran while one was open for 10% -> 0% of each run, Pallas kernels for 0% -> 0%
where the time goes in v1:
time: 70.1 us; the launch traced here: 68.9 us
  Pallas kernels  57.3 us (82%)
  local copies, waits for them, and re-layouts  11.6 us (17%)
    pallas_call x1, Pallas kernels, body(): pl.pallas_call(functools.partial(kernel, scale), out_shape=jax.ShapeDtype...  57.3 us
    unnamed x27, local copies, waits for them, and re-layouts  11.6 us

profile of v1, /device:TPU:6, one launch (start us, length us, event | category | flops | bytes accessed | tf_op | source)
XLA Modules:
  0.0 68.9 jit_solution(15267660205862676534)
XLA Ops:
  0.0 0.0 copy-start
  0.0 1.2 %copy-done = bf16[8,128,512]{2,1,0:T(8,128)(2,1)S(1)} copy-done((bf16[8,128,512]{2,1,0:T(8,128)(2,1)S(1)}, bf16[8,128,512]{2,1,0:T(8,128)(2,1)}, u32[]{:S(2)}) %copy-start) | copy-done | bytes 1048600
  1.2 0.0 copy-start.1
  1.2 1.2 %copy-done.1 = bf16[8,512,128]{2,1,0:T(8,128)(2,1)S(1)} copy-done((bf16[8,512,128]{2,1,0:T(8,128)(2,1)S(1)}, bf16[8,512,128]{2,1,0:T(8,128)(2,1)}, u32[]{:S(2)}) %copy-start.1) | copy-done | bytes 1048600
  2.5 0.0 copy-start.2
  2.5 1.0 %copy-done.2 = bf16[2,256,512]{2,1,0:T(8,128)(2,1)S(1)} copy-done((bf16[2,256,512]{2,1,0:T(8,128)(2,1)S(1)}, bf16[2,256,512]{2,1,0:T(8,128)(2,1)}, u32[]{:S(2)}) %copy-start.2) | copy-done | bytes 524312
  3.5 0.0 copy-start.3
  3.5 1.0 %copy-done.3 = bf16[2,256,512]{2,1,0:T(8,128)(2,1)S(1)} copy-done((bf16[2,256,512]{2,1,0:T(8,128)(2,1)S(1)}, bf16[2,256,512]{2,1,0:T(8,128)(2,1)}, u32[]{:S(2)}) %copy-start.3) | copy-done | bytes 524312
  4.5 0.0 copy-start.4
  4.5 0.8 %copy-done.4 = bf16[2,64,256]{2,1,0:T(8,128)(2,1)S(1)} copy-done((bf16[2,64,256]{2,1,0:T(8,128)(2,1)S(1)}, bf16[2,64,256]{2,1,0:T(8,128)(2,1)}, u32[]{:S(2)}) %copy-start.4) | copy-done | bytes 65560
  5.4 0.0 copy-start.5
  5.4 0.8 %copy-done.5 = bf16[2,64,256]{2,1,0:T(8,128)(2,1)S(1)} copy-done((bf16[2,64,256]{2,1,0:T(8,128)(2,1)S(1)}, bf16[2,64,256]{2,1,0:T(8,128)(2,1)}, u32[]{:S(2)}) %copy-start.5) | copy-done | bytes 65560
  6.2 0.0 copy-start.6
  6.2 0.7 %copy-done.6 = bf16[4,2,8,128]{3,2,1,0:T(8,128)(2,1)S(1)} copy-done((bf16[4,2,8,128]{3,2,1,0:T(8,128)(2,1)S(1)}, bf16[4,2,8,128]{3,2,1,0:T(8,128)(2,1)}, u32[]{:S(2)}) %copy-start.6) | copy-done | bytes 16408
  6.9 0.0 copy-start.7
  6.9 0.7 %copy-done.7 = bf16[4,2,8,64]{3,2,1,0:T(8,128)(2,1)S(1)} copy-done((bf16[4,2,8,64]{3,2,1,0:T(8,128)(2,1)S(1)}, bf16[4,2,8,64]{3,2,1,0:T(8,128)(2,1)}, u32[]{:S(2)}) %copy-start.7) | copy-done | bytes 8216
  7.7 0.0 copy-start.8
  7.7 0.7 %copy-done.8 = bf16[4,2,512]{2,1,0:T(2,128)(2,1)S(1)} copy-done((bf16[4,2,512]{2,1,0:T(2,128)(2,1)S(1)}, bf16[4,2,512]{2,1,0:T(2,128)(2,1)}, u32[]{:S(2)}) %copy-start.8) | copy-done | bytes 8216
  8.3 0.0 copy-start.9
  8.4 0.7 copy-done.9
  9.0 0.0 copy-start.10
  9.0 0.7 copy-done.10
  9.7 0.0 copy-start.11
  9.7 0.7 copy-done.11
  10.3 0.0 copy-start.12
  10.3 0.7 copy-done.12
  11.0 57.3 %latent_attend.1 = bf16[4,2,8,128]{3,2,1,0:T(8,128)(2,1)S(1)} custom-call(bf16[2,256,512]{2,1,0:T(8,128)(2,1)S(1)} %copy-done.2, bf16[2,64,256]{2,1,0:T(8,128)(2,1)S(1)} %copy-done.4, s32[1,2]{1,0:T(1,128)S(1)} %copy-done.10, s32[1,2]{1,0:T(1,128)S(1)} %copy-done.11, bf16[2,256,512]{2,1,0:T(8,128)(2,1)S(1)} %copy-done.3, bf16[2,64,256]{2,1,0:T(8,128)(2,1)S(1)} %copy-done.5, ...), custom_call_target="tpu_custom_call" | custom-call | tf_op jit(solution)/shard_map/latent_attend/pallas_call | solution.py:431
  68.3 0.6 copy.15
Async XLA Ops:
  0.0 1.2 %copy-start = (bf16[8,128,512]{2,1,0:T(8,128)(2,1)S(1)}, bf16[8,128,512]{2,1,0:T(8,128)(2,1)}, u32[]{:S(2)}) copy-start(bf16[8,128,512]{2,1,0:T(8,128)(2,1)} %kup_hbm.1) | copy-start | bytes 3145732
  1.2 1.2 %copy-start.1 = (bf16[8,512,128]{2,1,0:T(8,128)(2,1)S(1)}, bf16[8,512,128]{2,1,0:T(8,128)(2,1)}, u32[]{:S(2)}) copy-start(bf16[8,512,128]{2,1,0:T(8,128)(2,1)} %vup_hbm.1) | copy-start | bytes 3145732
  2.5 1.0 %copy-start.2 = (bf16[2,256,512]{2,1,0:T(8,128)(2,1)S(1)}, bf16[2,256,512]{2,1,0:T(8,128)(2,1)}, u32[]{:S(2)}) copy-start(bf16[2,256,512]{2,1,0:T(8,128)(2,1)} %plat_hbm.1) | copy-start | bytes 1572868
  3.5 1.0 %copy-start.3 = (bf16[2,256,512]{2,1,0:T(8,128)(2,1)S(1)}, bf16[2,256,512]{2,1,0:T(8,128)(2,1)}, u32[]{:S(2)}) copy-start(bf16[2,256,512]{2,1,0:T(8,128)(2,1)} %rlat_hbm.1) | copy-start | bytes 1572868
  4.5 0.8 %copy-start.4 = (bf16[2,64,256]{2,1,0:T(8,128)(2,1)S(1)}, bf16[2,64,256]{2,1,0:T(8,128)(2,1)}, u32[]{:S(2)}) copy-start(bf16[2,64,256]{2,1,0:T(8,128)(2,1)} %prope.1) | copy-start | bytes 196612
  5.4 0.8 %copy-start.5 = (bf16[2,64,256]{2,1,0:T(8,128)(2,1)S(1)}, bf16[2,64,256]{2,1,0:T(8,128)(2,1)}, u32[]{:S(2)}) copy-start(bf16[2,64,256]{2,1,0:T(8,128)(2,1)} %rrope.1) | copy-start | bytes 196612
  6.2 0.7 %copy-start.6 = (bf16[4,2,8,128]{3,2,1,0:T(8,128)(2,1)S(1)}, bf16[4,2,8,128]{3,2,1,0:T(8,128)(2,1)}, u32[]{:S(2)}) copy-start(bf16[4,2,8,128]{3,2,1,0:T(8,128)(2,1)} %qn.1) | copy-start | bytes 49156
  6.9 0.7 %copy-start.7 = (bf16[4,2,8,64]{3,2,1,0:T(8,128)(2,1)S(1)}, bf16[4,2,8,64]{3,2,1,0:T(8,128)(2,1)}, u32[]{:S(2)}) copy-start(bf16[4,2,8,64]{3,2,1,0:T(8,128)(2,1)} %qr.1) | copy-start | bytes 24580
  7.7 0.7 %copy-start.8 = (bf16[4,2,512]{2,1,0:T(2,128)(2,1)S(1)}, bf16[4,2,512]{2,1,0:T(2,128)(2,1)}, u32[]{:S(2)}) copy-start(bf16[4,2,512]{2,1,0:T(2,128)(2,1)} %nlat.1) | copy-start | bytes 24580
  8.3 0.7 copy-start.9
  9.0 0.7 copy-start.10
  9.7 0.7 copy-start.11
  10.3 0.7 copy-start.12

commit v2 on v1

--- a/solution.py
+++ b/solution.py
@@ -129,9 +129,10 @@
 
 def kernel(
     scale,
-    plat_hbm, prope, plen, dest, rlat_hbm, rrope, rlen, nlat, nrope, qn, qr, kup_hbm, vup_hbm,
+    plat_hbm, prope_hbm, plen_hbm, dest_hbm, rlat_hbm, rrope_hbm, rlen_hbm, nlat_hbm, nrope_hbm,
+    qn_hbm, qr_hbm, kup_hbm, vup_hbm,
     out,
-    plat, rlat, kup, vup, aux, pay, xsend, xrecv, g_res, g_inc,
+    plat, prope, plen, dest, rlat, rrope, rlen, nlat, nrope, qn, qr, kup, vup, aux, pay, xsend, xrecv, g_res, g_inc,
     obf, ost, sib_bf, sib_st, zs_bf, zs_st, zr_bf, zr_st, ret_send, ret_recv, small,
     load_sem, aux_ss, aux_rs, y_ss, y_rs, x_ss, x_rs, gz_ss, gz_rs, gs_ss, gs_rs,
     cs_ss, cs_rs, zo_ss, zo_rs, zt_ss, zt_rs, ret_ss, ret_rs,
@@ -145,9 +146,49 @@
     loads = [
         pltpu.make_async_copy(src, dst, load_sem.at[i])
         for i, (src, dst) in enumerate(
-            [(kup_hbm, kup), (rlat_hbm, rlat), (plat_hbm, plat), (vup_hbm, vup)]
+            [
+                (qn_hbm, qn), (qr_hbm, qr), (nlat_hbm, nlat), (nrope_hbm, nrope), (dest_hbm, dest),
+                (kup_hbm, kup),
+                (rlat_hbm, rlat), (rrope_hbm, rrope), (rlen_hbm, rlen),
+                (plat_hbm, plat), (prope_hbm, prope), (plen_hbm, plen),
+                (vup_hbm, vup),
+            ]
         )
     ]
+    need_small, need_kup, need_res, need_inc, need_vup = (
+        loads[0:5], loads[5:6], loads[6:9], loads[9:12], loads[12:13]
+    )
+
+    waiting = list(loads)
+
+    def arrive(wanted):
+        for load in wanted:
+            load.wait()
+            waiting.remove(load)
+
+    sent = []
+
+    def send(copy):
+        copy.start()
+        sent.append(copy)
+
+    def over_groups(start):
+        def step(k, _):
+            start((g + k) % NG)
+            return 0
+
+        lax.fori_loop(1, NG, step, 0)
+
+    sent_over_groups = []
+
+    def drain():
+        for load in waiting:
+            load.wait()
+        for copy in sent:
+            copy.wait_send()
+        if sent_over_groups:
+            over_groups(lambda to: [copy(to, g).wait_send() for copy in sent_over_groups])
+
     for load in loads:
         load.start()
 
@@ -167,6 +208,7 @@
             src_ref=src, dst_ref=dst, send_sem=ss, recv_sem=rs, device_id=device, device_id_type=MESH
         )
 
+    arrive(need_small)
     qn_all = qn[...].astype(F32).reshape(64, 128)
     qr_all = qr[...].astype(F32).reshape(64, 64)
     fresh_all = nlat[...].astype(F32)
@@ -192,17 +234,14 @@
         return remote(pay.at[y], pay.at[y], y_ss.at[to], y_rs.at[frm], (x * NY + to, d))
 
     for k in range(1, NY):
-        y_copy((y + k) % NY, y).start()
+        send(y_copy((y + k) % NY, y))
 
     def aux_copy(to, frm):
         ref = aux.at[pl.ds(g * 2, 2)]
         return remote(ref, ref, aux_ss.at[to], aux_rs.at[frm], (to, d))
 
-    def send_aux(k, _):
-        aux_copy((g + k) % NG, g).start()
-        return 0
-
-    lax.fori_loop(1, NG, send_aux, 0)
+    over_groups(lambda to: aux_copy(to, g).start())
+    sent_over_groups.append(aux_copy)
 
     def gather_start(p, gathered, absorbed, ropes):
         for k in range(4):
@@ -210,8 +249,8 @@
         gathered[mine, 128:144, :] = jnp.concatenate(ropes, axis=1).astype(BF16)
         for k in range(1, NZ):
             to = (z + k) % NZ
-            gather_z(p, gathered, to, z).start()
-        gather_sib(p, gathered, z).start()
+            send(gather_z(p, gathered, to, z))
+        send(gather_sib(p, gathered, z))
 
     def gather_z(p, gathered, to, frm):
         ref = gathered.at[mine]
@@ -225,13 +264,13 @@
         for k in (1, 7, 2, 6, 3, 5, 4):
             frm = (z + k) % NZ
             gather_z(p, gathered, frm, frm).wait_recv()
-            gather_sib(p, gathered, frm).start()
+            send(gather_sib(p, gathered, frm))
 
     def gather_finish(p, gathered):
         for frm in range(NZ):
             gather_sib(p, gathered, frm).wait_recv()
 
-    loads[0].wait()
+    arrive(need_kup)
     absorbed_res = absorb(qn_all[0:32].astype(BF16), kup)
     ropes_res = [qr_all[0:16], qr_all[16:32]]
     gather_start(0, g_res, absorbed_res, ropes_res)
@@ -243,12 +282,7 @@
         frm = (y + k) % NY
         y_copy(frm, frm).wait_recv()
 
-    def wait_aux(k, _):
-        frm = (g + k) % NG
-        aux_copy(frm, frm).wait_recv()
-        return 0
-
-    lax.fori_loop(1, NG, wait_aux, 0)
+    over_groups(lambda frm: aux_copy(frm, frm).wait_recv())
 
     def x_copy(to, frm):
         return remote(xsend.at[to], xrecv.at[x], x_ss.at[to], x_rs.at[frm], (to * NY + y, d))
@@ -268,7 +302,7 @@
             else:
                 xrecv[x, r] = block.astype(BF16)
         if k:
-            x_copy(to, x).start()
+            send(x_copy(to, x))
 
     gather_forward(0, g_res)
 
@@ -314,7 +348,7 @@
     def partials(p, gathered, latent, rope, lengths):
         attend(scale, gathered, latent, rope, lengths, offset, obf.at[p], ost.at[p])
         for copy in cores_copy(p):
-            copy.start()
+            send(copy)
 
     def exchange(p):
         for copy in cores_copy(p):
@@ -326,7 +360,7 @@
         )
         for k in (4, 3, 5, 2, 6, 1, 7):
             for copy in out_copy(p, (z + k) % NZ, z):
-                copy.start()
+                send(copy)
         zr_bf[p, z] = zs_bf[p, z]
         zr_st[p, z] = zs_st[p, z]
 
@@ -337,16 +371,16 @@
                 copy.wait_recv()
 
     gather_finish(0, g_res)
-    loads[1].wait()
+    arrive(need_res)
     partials(0, g_res, rlat, rrope, [rlen[0, 0], rlen[0, 1]])
     gather_forward(1, g_inc)
     exchange(0)
     gather_finish(1, g_inc)
-    loads[2].wait()
+    arrive(need_inc)
     partials(1, g_inc, plat, prope, [plen[0, 0], plen[0, 1]])
     exchange(1)
 
-    loads[3].wait()
+    arrive(need_vup)
     collect(0)
     out_res = finish(zr_bf.at[0], zr_st.at[0], scores_res, fresh_res, vup)
     out[0:2] = out_res.reshape(2, 2, 8, 128).astype(BF16)
@@ -366,21 +400,15 @@
     def ret_copy(to, frm):
         return remote(ret_send.at[to], ret_recv.at[g], ret_ss.at[to], ret_rs.at[frm], (to, d))
 
-    def ret_start(k, _):
-        to = (g + k) % NG
+    def ret_start(to):
         ret_send[to] = ret_block(to)
         ret_copy(to, g).start()
-        return 0
-
-    lax.fori_loop(1, NG, ret_start, 0)
+
+    over_groups(ret_start)
+    sent_over_groups.append(ret_copy)
     ret_recv[g] = ret_block(g)
 
-    def ret_wait(k, _):
-        frm = (g + k) % NG
-        ret_copy(frm, frm).wait_recv()
-        return 0
-
-    lax.fori_loop(1, NG, ret_wait, 0)
+    over_groups(lambda frm: ret_copy(frm, frm).wait_recv())
 
     def choose(frm, chosen):
         block = ret_recv[frm].astype(F32)
@@ -396,27 +424,7 @@
     for i in range(2):
         out[2 + i] = chosen[i].reshape(2, 8, 128).astype(BF16)
 
-    def drain(k, _):
-        to = (g + k) % NG
-        aux_copy(to, g).wait_send()
-        ret_copy(to, g).wait_send()
-        return 0
-
-    lax.fori_loop(1, NG, drain, 0)
-    for k in range(1, NY):
-        y_copy((y + k) % NY, y).wait_send()
-    for k in range(1, NX):
-        x_copy((x + k) % NX, x).wait_send()
-    for p, gathered in ((0, g_res), (1, g_inc)):
-        for k in range(1, NZ):
-            to = (z + k) % NZ
-            gather_z(p, gathered, to, z).wait_send()
-            for copy in out_copy(p, to, z):
-                copy.wait_send()
-        for frm in range(NZ):
-            gather_sib(p, gathered, frm).wait_send()
-        for copy in cores_copy(p):
-            copy.wait_send()
+    drain()
 
 
 def body(
@@ -425,17 +433,25 @@
 ):
     scale = attend_scale(query_nope.shape[-1], query_rope.shape[-1])
     vmem = pl.BlockSpec(memory_space=pltpu.VMEM)
-    smem = pl.BlockSpec(memory_space=pltpu.SMEM)
-    hbm = pl.BlockSpec(memory_space=pl.ANY)
+    hbm = pl.BlockSpec(memory_space=pltpu.HBM)
     dma = pltpu.SemaphoreType.DMA
     return pl.pallas_call(
         functools.partial(kernel, scale),
         out_shape=jax.ShapeDtypeStruct((4, 2, 8, 128), BF16),
-        in_specs=[hbm, vmem, smem, smem, hbm, vmem, smem, vmem, vmem, vmem, vmem, hbm, hbm],
+        in_specs=[hbm] * 13,
         out_specs=vmem,
         scratch_shapes=[
             pltpu.VMEM((2, 256, 512), BF16),
+            pltpu.VMEM((2, 64, 256), BF16),
+            pltpu.SMEM((1, 2), jnp.int32),
+            pltpu.SMEM((1, 2), jnp.int32),
             pltpu.VMEM((2, 256, 512), BF16),
+            pltpu.VMEM((2, 64, 256), BF16),
+            pltpu.SMEM((1, 2), jnp.int32),
+            pltpu.VMEM((4, 2, 512), BF16),
+            pltpu.VMEM((4, 2, 64), BF16),
+            pltpu.VMEM((4, 2, 8, 128), BF16),
+            pltpu.VMEM((4, 2, 8, 64), BF16),
             pltpu.VMEM((8, 128, 512), BF16),
             pltpu.VMEM((8, 512, 128), BF16),
             pltpu.VMEM((NG * 2, 2, 128), F32),
@@ -455,7 +471,7 @@
             pltpu.VMEM((NG, 16, 128), BF16),
             pltpu.VMEM((NG, 16, 128), BF16),
             pltpu.VMEM((8, 128), F32),
-            dma((4,)),
+            dma((13,)),
             dma((NG,)), dma((NG,)),
             dma((NY,)), dma((NY,)),
             dma((NX,)), dma((NX,)),
@@ -470,10 +486,10 @@
             collective_id=0, has_side_effects=True, vmem_limit_bytes=48 << 20
         ),
         name="latent_attend",
-    )(
+    )(*(pltpu.with_memory_space_constraint(a, pltpu.HBM) for a in (
         prompt_latent_cache, prompt_rope, prompt_length, dest_slot, resident_latent, resident_rope,
         resident_length, new_latent, new_rope, query_nope, query_rope, key_up, value_up_weight,
-    )
+    )))
 
 
 def solution(mesh):

time: 70.1 us -> 58 us (0.83)
  local copies, waits for them, and re-layouts: 11.6 us -> 0.61 us
    unnamed x27 -> x1, local copies, waits for them, and re-layouts: 11.6 us -> 0.61 us
where the time goes in v2:
time: 58 us; the launch traced here: 57.4 us
  Pallas kernels  56.8 us (98%)
  local copies, waits for them, and re-layouts  0.61 us (1%)
    pallas_call x1, Pallas kernels, body(): pl.pallas_call(functools.partial(kernel, scale), out_shape=jax.ShapeDtype...  56.8 us

profile of v2, /device:TPU:6, one launch (start us, length us, event | category | flops | bytes accessed | tf_op | source)
XLA Modules:
  0.0 57.4 jit_solution(1965860312251525241)
XLA Ops:
  0.0 56.8 %latent_attend.1 = bf16[4,2,8,128]{3,2,1,0:T(8,128)(2,1)S(1)} custom-call(bf16[2,256,512]{2,1,0:T(8,128)(2,1)} %plat_hbm.1, bf16[2,64,256]{2,1,0:T(8,128)(2,1)} %prope_hbm.1, s32[1,2]{1,0:T(1,128)} %plen_hbm.1, s32[1,2]{1,0:T(1,128)} %dest_hbm.1, bf16[2,256,512]{2,1,0:T(8,128)(2,1)} %rlat_hbm.1, bf16[2,64,256]{2,1,0:T(8,128)(2,1)} %rrope_hbm.1, ...), custom_call_target="tpu_custom_call" | custom-call | tf_op jit(solution)/shard_map/latent_attend/pallas_call | solution.py:438
  56.8 0.6 %copy.15 = bf16[4,2,8,128]{3,2,1,0:T(8,128)(2,1)} copy(bf16[4,2,8,128]{3,2,1,0:T(8,128)(2,1)S(1)} %latent_attend.1) | data formatting | bytes 32768

commit v3 on v2

v3 whole, which is shorter than its diff:
```python
import functools
import math

import jax
import jax.numpy as jnp
from jax import lax
from jax.experimental import pallas as pl
from jax.experimental.pallas import tpu as pltpu
from jax.sharding import PartitionSpec as P

MESH = pl.DeviceIdType.MESH
F32 = jnp.float32
BF16 = jnp.bfloat16
NX, NY, NZ = 4, 8, 8
NG = NX * NY
NEG = -1e30


def attend_scale(nope_width, rotary_width):
    return (0.1 * math.log(40.0) + 1.0) ** 2 / math.sqrt(nope_width + rotary_width)


def iota(shape, axis):
    return lax.broadcasted_iota(jnp.int32, shape, axis)


def columns_of(rows, field):
    n = rows.shape[0]
    hit = iota((n, 16, 128), 2) == iota((n, 16, 128), 1) + 16 * field
    return jnp.sum(jnp.where(hit, jnp.broadcast_to(rows, (n, 16, 128)), 0.0), axis=-1, keepdims=True)


def rows_of(fields):
    n = fields[0].shape[0]
    lane, sub = iota((n, 16, 128), 2), iota((n, 16, 128), 1)
    packed = jnp.zeros((n, 16, 128), F32)
    for f, column in enumerate(fields):
        packed = jnp.where(lane == sub + 16 * f, jnp.broadcast_to(column, (n, 16, 128)), packed)
    return jnp.sum(packed, axis=1, keepdims=True)


def absorb(q32, kup):
    head = iota((32, 512), 0) % 8
    total = jnp.zeros((32, 512), F32)
    for h in range(8):
        total = jnp.where(head == h, jnp.dot(q32, kup[h], preferred_element_type=F32), total)
    return total.astype(BF16)


def new_scores(scale, absorbed, ropes, fresh, fresh_rope):
    step = iota((16, 1), 0) // 8
    out = []
    for s in range(2):
        q = absorbed[s * 16 : (s + 1) * 16].astype(F32)
        pair = []
        for n in range(2):
            v = jnp.sum(q * fresh[s][n], axis=-1, keepdims=True)
            v = v + jnp.sum(ropes[s] * fresh_rope[s][n], axis=-1, keepdims=True)
            v = v * scale
            pair.append(v if n == 0 else jnp.where(step >= 1, v, NEG))
        out.append(pair)
    return out


def attend(scale, gathered, keys, rope, length, offset, out_bf):
    q = jnp.concatenate(
        [gathered[:, k * 16 : (k + 1) * 16, :].reshape(128, 128) for k in range(4)], axis=1
    )
    ropes = gathered[:, 64:80, :].reshape(128, 128)[:, 0:64]
    scores = lax.dot_general(q, keys, (((1,), (1,)), ((), ())), preferred_element_type=F32)
    scores = scale * (scores + jnp.dot(ropes, rope, preferred_element_type=F32))
    live = offset + iota((128, 512), 1) < length
    scores = jnp.where(live, scores, NEG)
    top = jnp.max(scores, axis=-1, keepdims=True)
    weights = jnp.where(live, jnp.exp(scores - top), 0.0)
    total = jnp.sum(weights, axis=-1, keepdims=True)
    summed = jnp.dot(weights.astype(BF16), keys, preferred_element_type=F32)
    summed = summed / jnp.maximum(total, 1.0)
    out_bf[...] = summed.reshape(8, 16, 512).astype(BF16)
    return top.reshape(8, 16, 1), total.reshape(8, 16, 1)


def finish(blocks, stats, fresh_scores, fresh, vup):
    rows = []
    for s in range(2):
        m, l = columns_of(stats[...], s), columns_of(stats[...], 2 + s)
        n0, n1 = fresh_scores[s]
        top = jnp.maximum(jnp.max(m, axis=0), jnp.maximum(n0, n1))
        w = l * jnp.exp(m - top[None])
        w0 = jnp.exp(n0 - top)
        w1 = jnp.where(n1 > NEG, jnp.exp(n1 - top), 0.0)
        under = jnp.sum(w, axis=0) + w0 + w1
        total = w0 * fresh[s][0] + w1 * fresh[s][1]
        for j in range(NZ):
            total = total + w[j] * blocks[s, j].astype(F32)
        rows.append(total / under)
    attended = jnp.concatenate(rows, axis=0).astype(BF16)
    head = iota((32, 128), 0) % 8
    out = jnp.zeros((32, 128), F32)
    for h in range(8):
        out = jnp.where(head == h, jnp.dot(attended, vup[h], preferred_element_type=F32), out)
    return out


def kernel(
    scale,
    plat_hbm, prope_hbm, plen_hbm, dest_hbm, rlat_hbm, rrope_hbm, rlen_hbm, nlat_hbm, nrope_hbm,
    qn_hbm, qr_hbm, kup_hbm, vup_hbm,
    out,
    lat, rope, plen, dest, rlen, nlat, nrope, qn, qr, kup, vup,
    dest_x, dest_all, pay_a, pay_b, xs_a, xs_b, xr_a, xr_b, gathered,
    zs_bf, zs_st, zr_bf, zr_st, ret_send, ret_recv, small,
    load_sem, sib_ss, sib_rs, ya_ss, ya_rs, yb_ss, yb_rs, xa_ss, xa_rs, xb_ss, xb_rs,
    dx_ss, dx_rs, da_ss, da_rs, gz_ss, gz_rs, zo_ss, zo_rs, zt_ss, zt_rs, ret_ss, ret_rs,
):
    g, d = lax.axis_index("grp"), lax.axis_index("dev")
    x, y = g // NY, g % NY
    z, c = d // 2, d % 2

    def along_z(k):
        return (g, ((z + k + NZ) % NZ) * 2 + c)

    def along_y(k):
        return (x * NY + (y + k) % NY, d)

    def along_x(k):
        return (((x + k) % NX) * NY + y, d)

    sibling = (g, z * 2 + 1 - c)

    barrier = pltpu.get_barrier_semaphore()
    peers = [along_y(k) for k in range(1, NY)] + [along_x(k) for k in range(1, NX)]
    peers += [sibling] + [along_z(k) for k in range(1, NZ)]
    for peer in peers:
        pl.semaphore_signal(barrier, inc=1, device_id=peer, device_id_type=MESH)

    half = pl.ds(pl.multiple_of(c * 256, 256), 256)
    loads = [
        pltpu.make_async_copy(src, dst, load_sem.at[i])
        for i, (src, dst) in enumerate(
            [
                (qn_hbm, qn), (qr_hbm, qr), (nlat_hbm, nlat), (nrope_hbm, nrope), (dest_hbm, dest),
                (kup_hbm, kup),
                (rlat_hbm, lat.at[0, :, half, :]), (rrope_hbm, rope.at[0, :, :, half]), (rlen_hbm, rlen),
                (plat_hbm, lat.at[1, :, half, :]), (prope_hbm, rope.at[1, :, :, half]), (plen_hbm, plen),
                (vup_hbm, vup),
            ]
        )
    ]
    need_small, need_kup, need_res, need_inc, need_vup = (
        loads[0:5], loads[5:6], loads[6:9], loads[9:12], loads[12:13]
    )
    for load in loads:
        load.start()
    waiting = list(loads)

    def arrive(wanted):
        for load in wanted:
            load.wait()
            waiting.remove(load)

    sent = []

    def send(copy):
        copy.start()
        sent.append(copy)

    def over_groups(start):
        def step(k, _):
            start((g + k) % NG)
            return 0

        lax.fori_loop(1, NG, step, 0)

    sent_over_groups = []

    def drain():
        for load in waiting:
            load.wait()
        for copy in sent:
            copy.wait_send()
        if sent_over_groups:
            over_groups(lambda to: [copy(to, g).wait_send() for copy in sent_over_groups])

    def remote(src, dst, ss, rs, device):
        return pltpu.make_async_remote_copy(
            src_ref=src, dst_ref=dst, send_sem=ss, recv_sem=rs, device_id=device, device_id_type=MESH
        )

    def sib_copies(p):
        lat_hbm, rope_hbm = ((rlat_hbm, rrope_hbm), (plat_hbm, prope_hbm))[p]
        return (
            remote(lat_hbm, lat.at[p, :, half, :], sib_ss.at[p, 0], sib_rs.at[p, 0], sibling),
            remote(rope_hbm, rope.at[p, :, :, half], sib_ss.at[p, 1], sib_rs.at[p, 1], sibling),
        )

    arrive(need_small)
    qn_all = qn[...].astype(F32).reshape(64, 128)
    qr_all = qr[...].astype(F32).reshape(64, 64)
    fresh_all = nlat[...].astype(F32)
    fresh_rope_all = nrope[...].astype(F32)
    rope_rows = [
        jnp.concatenate([qr_all[s * 16 : s * 16 + 8], qr_all[s * 16 + 8 : s * 16 + 16]], axis=1)
        for s in (2, 3)
    ]
    pay_a[y] = jnp.concatenate([qn_all[32:64]] + rope_rows, axis=0).astype(BF16)
    for i in range(2):
        dest_x[x * 2 + i] = jnp.full((1, 128), dest[0, i].astype(F32))
        dest_all[g * 2 + i] = jnp.full((1, 128), dest[0, i].astype(F32))

    pl.semaphore_wait(barrier, len(peers))

    def ya_copy(to, frm):
        return remote(pay_a.at[y], pay_a.at[y], ya_ss.at[to], ya_rs.at[frm], (x * NY + to, d))

    def yb_copy(to, frm):
        return remote(pay_b.at[y], pay_b.at[y], yb_ss.at[to], yb_rs.at[frm], (x * NY + to, d))

    def dx_copy(to, frm):
        ref = dest_x.at[pl.ds(x * 2, 2)]
        return remote(ref, ref, dx_ss.at[to], dx_rs.at[frm], (to * NY + y, d))

    for k in (4, 3, 5, 2, 6, 1, 7):
        send(ya_copy((y + k) % NY, y))
    for k in range(1, NX):
        send(dx_copy((x + k) % NX, x))

    GATHER = ((0, 1), (0, -1), (0, 2), (0, -2), (-2, 1), (2, -1), (-2, 2), (2, -2))

    def part(p, s, chunk, kind):
        cut = 48 if s == 0 else 32
        ref = gathered.at[p, s, (z + chunk + NZ) % NZ]
        if kind == 6:
            return ref.at[pl.ds(0, cut)]
        if kind == 7:
            return ref.at[pl.ds(cut, 80 - cut)]
        return ref

    def gather_out(p, s, kind):
        chunk, by = GATHER[kind]
        ref = part(p, s, chunk, kind)
        return remote(ref, ref, gz_ss.at[p, s, kind], gz_rs.at[p, s, kind], along_z(by))

    def gather_in(p, s, kind):
        chunk, by = GATHER[kind]
        ref = part(p, s, chunk - by, kind)
        return remote(ref, ref, gz_ss.at[p, s, kind], gz_rs.at[p, s, kind], along_z(-by))

    def gather_start(p, absorbed, ropes):
        blank = jnp.zeros((16, 64), F32)
        for s in range(2):
            for k in range(4):
                gathered[p, s, z, k * 16 : (k + 1) * 16, :] = absorbed[
                    s * 16 : (s + 1) * 16, k * 128 : (k + 1) * 128
                ]
            gathered[p, s, z, 64:80, :] = jnp.concatenate([ropes[s], blank], axis=1).astype(BF16)
            for kind in (2, 3):
                send(gather_out(p, s, kind))
        for s in range(2):
            for kind in (0, 1):
                send(gather_out(p, s, kind))

    def gather_mid(p):
        for s in range(2):
            for kind in (2, 3):
                gather_in(p, s, kind).wait_recv()
                send(gather_out(p, s, kind + 2))
                send(gather_out(p, s, kind + 4))

    def gather_end(p, s):
        for kind in (0, 1, 4, 5, 6, 7):
            gather_in(p, s, kind).wait_recv()

    arrive(need_kup)
    absorbed_res = absorb(qn_all[0:32].astype(BF16), kup)
    ropes_res = [qr_all[0:16], qr_all[16:32]]
    gather_start(0, absorbed_res, ropes_res)
    for copy in sib_copies(0):
        send(copy)

    tokens = []
    for i in range(2):
        for n in range(2):
            for k in range(4):
                small[n * 4 + k : n * 4 + k + 1, :] = fresh_all[2 + i, n : n + 1, k * 128 : (k + 1) * 128]
        tokens.append(small[...])
    for i in range(2):
        row = jnp.concatenate([fresh_rope_all[2 + i, 0:1], fresh_rope_all[2 + i, 1:2]], axis=1)
        tokens.append(jnp.broadcast_to(row, (8, 128)))
    pay_b[y] = jnp.concatenate(tokens, axis=0).astype(BF16)
    for k in range(1, NY):
        send(yb_copy((y + k) % NY, y))
    for copy in sib_copies(1):
        send(copy)

    fresh_res = [[fresh_all[s, n : n + 1] for n in range(2)] for s in range(2)]
    fresh_rope_res = [[fresh_rope_all[s, n : n + 1] for n in range(2)] for s in range(2)]
    scores_res = new_scores(scale, absorbed_res, ropes_res, fresh_res, fresh_rope_res)

    def xa_copy(to, frm):
        return remote(xs_a.at[to], xr_a.at[x], xa_ss.at[to], xa_rs.at[frm], (to * NY + y, d))

    def xb_copy(to, frm):
        return remote(xs_b.at[to], xr_b.at[x], xb_ss.at[to], xb_rs.at[frm], (to * NY + y, d))

    def choose_for(to, held, base, width):
        blocks = []
        for r in range(2):
            wanted = dest_x[to * 2 + r]
            block = jnp.zeros((width, 128), F32)
            for j in range(NY):
                for i in range(2):
                    here = ((x * NY + j) * 2 + i).astype(F32)
                    rows = held[j, base + i * width : base + (i + 1) * width, :]
                    block = jnp.where(jnp.broadcast_to(wanted == here, (width, 128)), rows, block)
            blocks.append(block)
        return blocks

    for k in range(1, NY):
        frm = (y + k) % NY
        ya_copy(frm, frm).wait_recv()
    for k in range(1, NX):
        frm = (x + k) % NX
        dx_copy(frm, frm).wait_recv()
    held = pay_a[...].astype(F32)
    for k in (2, 1, 3, 0):
        to = (x + k) % NX
        block = choose_for(to, held, 0, 16) + choose_for(to, held, 32, 8)
        block = jnp.concatenate(block, axis=0).astype(BF16)
        if k:
            xs_a[to] = block
            send(xa_copy(to, x))
        else:
            xr_a[x] = block
    for k in range(1, NY):
        frm = (y + k) % NY
        yb_copy(frm, frm).wait_recv()
    held = pay_b[...].astype(F32)
    for k in (2, 1, 3, 0):
        to = (x + k) % NX
        block = choose_for(to, held, 0, 8) + choose_for(to, held, 16, 8)
        block = jnp.concatenate(block, axis=0).astype(BF16)
        if k:
            xs_b[to] = block
            send(xb_copy(to, x))
        else:
            xr_b[x] = block
    gather_mid(0)
    for k in range(1, NX):
        frm = (x + k) % NX
        xa_copy(frm, frm).wait_recv()
    block = xr_a[0].astype(F32)
    for j in range(1, NX):
        block = block + xr_a[j].astype(F32)
    ropes_inc = [
        jnp.concatenate([block[32 + 8 * r : 40 + 8 * r, 0:64], block[32 + 8 * r : 40 + 8 * r, 64:128]], axis=0)
        for r in range(2)
    ]
    absorbed_inc = absorb(block[0:32].astype(BF16), kup)
    gather_start(1, absorbed_inc, ropes_inc)

    def da_copy(to, frm):
        ref = dest_all.at[pl.ds(g * 2, 2)]
        return remote(ref, ref, da_ss.at[to], da_rs.at[frm], (to, d))

    over_groups(lambda to: da_copy(to, g).start())
    sent_over_groups.append(da_copy)

    for k in range(1, NX):
        frm = (x + k) % NX
        xb_copy(frm, frm).wait_recv()
    block = xr_b[0].astype(F32)
    for j in range(1, NX):
        block = block + xr_b[j].astype(F32)
    fresh_inc, fresh_rope_inc = [], []
    for r in range(2):
        small[...] = block[8 * r : 8 * r + 8]
        fresh_inc.append(
            [
                jnp.concatenate([small[n * 4 + k : n * 4 + k + 1, :] for k in range(4)], axis=1)
                for n in range(2)
            ]
        )
        row = block[16 + 8 * r : 17 + 8 * r]
        fresh_rope_inc.append([row[:, 0:64], row[:, 64:128]])
    scores_inc = new_scores(scale, absorbed_inc, ropes_inc, fresh_inc, fresh_rope_inc)

    def out_copy(p, s, to, frm):
        device = (g, to * 2 + c)
        return remote(zs_bf.at[p, s, to], zr_bf.at[p, s, z], zo_ss.at[p, s, to], zo_rs.at[p, s, frm], device)

    def stat_copy(p, to, frm):
        device = (g, to * 2 + c)
        return remote(zs_st.at[p, to], zr_st.at[p, z], zt_ss.at[p, to], zt_rs.at[p, frm], device)

    FAR_FIRST = (4, 3, 5, 2, 6, 1, 7)

    def partials(p, s, lengths):
        return attend(
            scale, gathered.at[p, s], lat[p, s], rope[p, s], lengths[0, s], z * 512, zs_bf.at[p, s]
        )

    def share(p, s):
        for k in FAR_FIRST:
            send(out_copy(p, s, (z + k) % NZ, z))
        zr_bf[p, s, z] = zs_bf[p, s, z]

    def share_stats(p, fields):
        zs_st[p] = rows_of([fields[0][0], fields[1][0], fields[0][1], fields[1][1]])
        for k in FAR_FIRST:
            send(stat_copy(p, (z + k) % NZ, z))
        zr_st[p, z] = zs_st[p, z]

    def collect(p):
        for k in FAR_FIRST:
            frm = (z + k) % NZ
            for s in range(2):
                out_copy(p, s, frm, frm).wait_recv()
            stat_copy(p, frm, frm).wait_recv()

    arrive(need_res)
    for copy in sib_copies(0):
        copy.wait_recv()
    fields_res = []
    for s in range(2):
        gather_end(0, s)
        fields_res.append(partials(0, s, rlen))
    gather_mid(1)
    arrive(need_inc)
    for copy in sib_copies(1):
        copy.wait_recv()
    fields_inc = []
    for s in range(2):
        gather_end(1, s)
        fields_inc.append(partials(1, s, plen))
        share(1, s)
    share_stats(1, fields_inc)
    arrive(need_vup)
    collect(1)
    for s in range(2):
        share(0, s)
    share_stats(0, fields_res)
    out_inc = finish(zr_bf.at[1], zr_st.at[1], scores_inc, fresh_inc, vup)

    def ret_block(to):
        block = jnp.zeros((16, 128), F32)
        for r in range(2):
            goal = dest_all[g * 2 + r]
            first = (to * 2).astype(F32)
            hit = (goal == first) | (goal == first + 1.0)
            block = jnp.where(jnp.broadcast_to(hit, (16, 128)), out_inc[r * 16 : (r + 1) * 16], block)
        return block.astype(BF16)

    def ret_copy(to, frm):
        return remote(ret_send.at[to], ret_recv.at[g], ret_ss.at[to], ret_rs.at[frm], (to, d))

    def ret_start(to):
        ret_send[to] = ret_block(to)
        ret_copy(to, g).start()

    over_groups(ret_start)
    sent_over_groups.append(ret_copy)
    ret_recv[g] = ret_block(g)

    collect(0)
    out_res = finish(zr_bf.at[0], zr_st.at[0], scores_res, fresh_res, vup)
    out[0:2] = out_res.reshape(2, 2, 8, 128).astype(BF16)

    over_groups(lambda frm: da_copy(frm, frm).wait_recv())
    over_groups(lambda frm: ret_copy(frm, frm).wait_recv())

    def choose(frm, chosen):
        block = ret_recv[frm].astype(F32)
        picked = []
        for i in range(2):
            here = (g * 2 + i).astype(F32)
            hit = (dest_all[frm * 2] == here) | (dest_all[frm * 2 + 1] == here)
            picked.append(jnp.where(jnp.broadcast_to(hit, (16, 128)), block, chosen[i]))
        return tuple(picked)

    zero = jnp.zeros((16, 128), F32)
    chosen = lax.fori_loop(0, NG, choose, (zero, zero))
    for i in range(2):
        out[2 + i] = chosen[i].reshape(2, 8, 128).astype(BF16)

    drain()


def body(
    prompt_latent_cache, prompt_rope, prompt_length, dest_slot, resident_latent, resident_rope,
    resident_length, new_latent, new_rope, query_nope, query_rope, key_up, value_up_weight,
):
    scale = attend_scale(query_nope.shape[-1], query_rope.shape[-1])
    hbm = pl.BlockSpec(memory_space=pltpu.HBM)
    dma = pltpu.SemaphoreType.DMA
    vmem = pltpu.VMEM
    return pl.pallas_call(
        functools.partial(kernel, scale),
        out_shape=jax.ShapeDtypeStruct((4, 2, 8, 128), BF16),
        in_specs=[hbm] * 13,
        out_specs=pl.BlockSpec(memory_space=pltpu.VMEM),
        scratch_shapes=[
            vmem((2, 2, 512, 512), BF16),
            vmem((2, 2, 64, 512), BF16),
            pltpu.SMEM((1, 2), jnp.int32),
            pltpu.SMEM((1, 2), jnp.int32),
            pltpu.SMEM((1, 2), jnp.int32),
            vmem((4, 2, 512), BF16),
            vmem((4, 2, 64), BF16),
            vmem((4, 2, 8, 128), BF16),
            vmem((4, 2, 8, 64), BF16),
            vmem((8, 128, 512), BF16),
            vmem((8, 512, 128), BF16),
            vmem((NX * 2, 1, 128), F32),
            vmem((NG * 2, 1, 128), F32),
            vmem((NY, 48, 128), BF16),
            vmem((NY, 32, 128), BF16),
            vmem((NX, 48, 128), BF16),
            vmem((NX, 32, 128), BF16),
            vmem((NX, 48, 128), BF16),
            vmem((NX, 32, 128), BF16),
            vmem((2, 2, NZ, 80, 128), BF16),
            vmem((2, 2, NZ, 16, 512), BF16),
            vmem((2, NZ, 1, 128), F32),
            vmem((2, 2, NZ, 16, 512), BF16),
            vmem((2, NZ, 1, 128), F32),
            vmem((NG, 16, 128), BF16),
            vmem((NG, 16, 128), BF16),
            vmem((8, 128), F32),
            dma((13,)),
            dma((2, 2)), dma((2, 2)),
            dma((NY,)), dma((NY,)), dma((NY,)), dma((NY,)),
            dma((NX,)), dma((NX,)), dma((NX,)), dma((NX,)),
            dma((NX,)), dma((NX,)),
            dma((NG,)), dma((NG,)),
            dma((2, 2, 8)), dma((2, 2, 8)),
            dma((2, 2, NZ)), dma((2, 2, NZ)),
            dma((2, NZ)), dma((2, NZ)),
            dma((NG,)), dma((NG,)),
        ],
        compiler_params=pltpu.CompilerParams(
            collective_id=0, has_side_effects=True, vmem_limit_bytes=48 << 20
        ),
        name="latent_attend",
    )(*(pltpu.with_memory_space_constraint(a, pltpu.HBM) for a in (
        prompt_latent_cache, prompt_rope, prompt_length, dest_slot, resident_latent, resident_rope,
        resident_length, new_latent, new_rope, query_nope, query_rope, key_up, value_up_weight,
    )))


def solution(mesh):
    placed = (
        P("grp", "dev", None),
        P("grp", None, "dev"),
        P("grp", None),
        P("grp", None),
        P("grp", "dev", None),
        P("grp", None, "dev"),
        P("grp", None),
        P("grp", None, None),
        P("grp", None, None),
        P("grp", None, "dev", None),
        P("grp", None, "dev", None),
        P("dev", None, None),
        P("dev", None, None),
    )
    return jax.shard_map(
        body, mesh=mesh, in_specs=placed, out_specs=P("grp", None, "dev", None), check_vma=False
    )
```

time: 58 us -> 55.1 us (0.950)
  the two profiles are of different devices: /device:TPU:6 before, /device:TPU:8 now
where the time goes in v3:
time: 55.1 us; the launch traced here: 55 us
  Pallas kernels  54.3 us (99%)
  local copies, waits for them, and re-layouts  0.61 us (1%)
    pallas_call x1, Pallas kernels, body(): pl.pallas_call(functools.partial(kernel, scale), out_shape=jax.ShapeDtype...  54.3 us

profile of v3, /device:TPU:8, one launch (start us, length us, event | category | flops | bytes accessed | tf_op | source)
XLA Modules:
  0.0 55.0 jit_solution(1504982838177657669)
XLA Ops:
  0.0 54.3 %latent_attend.1 = bf16[4,2,8,128]{3,2,1,0:T(8,128)(2,1)S(1)} custom-call(bf16[2,256,512]{2,1,0:T(8,128)(2,1)} %plat_hbm.1, bf16[2,64,256]{2,1,0:T(8,128)(2,1)} %prope_hbm.1, s32[1,2]{1,0:T(1,128)} %plen_hbm.1, s32[1,2]{1,0:T(1,128)} %dest_hbm.1, bf16[2,256,512]{2,1,0:T(8,128)(2,1)} %rlat_hbm.1, bf16[2,64,256]{2,1,0:T(8,128)(2,1)} %rrope_hbm.1, ...), custom_call_target="tpu_custom_call" | custom-call | tf_op jit(solution)/shard_map/latent_attend/pallas_call | solution.py:497
  54.3 0.6 %copy.15 = bf16[4,2,8,128]{3,2,1,0:T(8,128)(2,1)} copy(bf16[4,2,8,128]{3,2,1,0:T(8,128)(2,1)S(1)} %latent_attend.1) | data formatting | bytes 32768

commit v4 on v3

--- a/solution.py
+++ b/solution.py
@@ -172,15 +172,15 @@
 
         lax.fori_loop(1, NG, step, 0)
 
-    sent_over_groups = []
+    all_sent = []
 
     def drain():
         for load in waiting:
             load.wait()
         for copy in sent:
             copy.wait_send()
-        if sent_over_groups:
-            over_groups(lambda to: [copy(to, g).wait_send() for copy in sent_over_groups])
+        for copy in all_sent:
+            copy.wait_send()
 
     def remote(src, dst, ss, rs, device):
         return pltpu.make_async_remote_copy(
@@ -359,12 +359,13 @@
     absorbed_inc = absorb(block[0:32].astype(BF16), kup)
     gather_start(1, absorbed_inc, ropes_inc)
 
-    def da_copy(to, frm):
+    def da_copy(to):
         ref = dest_all.at[pl.ds(g * 2, 2)]
-        return remote(ref, ref, da_ss.at[to], da_rs.at[frm], (to, d))
-
-    over_groups(lambda to: da_copy(to, g).start())
-    sent_over_groups.append(da_copy)
+        return remote(ref, ref, da_ss, da_rs, (to, d))
+
+    over_groups(lambda to: da_copy(to).start())
+    da_every = remote(dest_all.at[pl.ds(0, 62)], dest_all.at[pl.ds(0, 62)], da_ss, da_rs, along_y(1))
+    all_sent.append(da_every)
 
     for k in range(1, NX):
         frm = (x + k) % NX
@@ -426,6 +427,7 @@
         gather_end(0, s)
         fields_res.append(partials(0, s, rlen))
     gather_mid(1)
+    share(0, 0)
     arrive(need_inc)
     for copy in sib_copies(1):
         copy.wait_recv()
@@ -435,11 +437,10 @@
         fields_inc.append(partials(1, s, plen))
         share(1, s)
     share_stats(1, fields_inc)
+    share(0, 1)
+    share_stats(0, fields_res)
     arrive(need_vup)
     collect(1)
-    for s in range(2):
-        share(0, s)
-    share_stats(0, fields_res)
     out_inc = finish(zr_bf.at[1], zr_st.at[1], scores_inc, fresh_inc, vup)
 
     def ret_block(to):
@@ -451,23 +452,21 @@
             block = jnp.where(jnp.broadcast_to(hit, (16, 128)), out_inc[r * 16 : (r + 1) * 16], block)
         return block.astype(BF16)
 
-    def ret_copy(to, frm):
-        return remote(ret_send.at[to], ret_recv.at[g], ret_ss.at[to], ret_rs.at[frm], (to, d))
-
     def ret_start(to):
         ret_send[to] = ret_block(to)
-        ret_copy(to, g).start()
+        remote(ret_send.at[to], ret_recv.at[g], ret_ss, ret_rs, (to, d)).start()
 
     over_groups(ret_start)
-    sent_over_groups.append(ret_copy)
+    ret_every = remote(ret_send.at[pl.ds(0, 31)], ret_recv.at[pl.ds(0, 31)], ret_ss, ret_rs, along_y(1))
+    all_sent.append(ret_every)
     ret_recv[g] = ret_block(g)
 
     collect(0)
     out_res = finish(zr_bf.at[0], zr_st.at[0], scores_res, fresh_res, vup)
     out[0:2] = out_res.reshape(2, 2, 8, 128).astype(BF16)
 
-    over_groups(lambda frm: da_copy(frm, frm).wait_recv())
-    over_groups(lambda frm: ret_copy(frm, frm).wait_recv())
+    da_every.wait_recv()
+    ret_every.wait_recv()
 
     def choose(frm, chosen):
         block = ret_recv[frm].astype(F32)
@@ -532,11 +531,11 @@
             dma((NY,)), dma((NY,)), dma((NY,)), dma((NY,)),
             dma((NX,)), dma((NX,)), dma((NX,)), dma((NX,)),
             dma((NX,)), dma((NX,)),
-            dma((NG,)), dma((NG,)),
+            dma, dma,
             dma((2, 2, 8)), dma((2, 2, 8)),
             dma((2, 2, NZ)), dma((2, 2, NZ)),
             dma((2, NZ)), dma((2, NZ)),
-            dma((NG,)), dma((NG,)),
+            dma, dma,
         ],
         compiler_params=pltpu.CompilerParams(
             collective_id=0, has_side_effects=True, vmem_limit_bytes=48 << 20

time: 55.1 us -> 50.8 us (0.922)
  the two profiles are of different devices: /device:TPU:8 before, /device:TPU:6 now
where the time goes in v4:
time: 50.8 us; the launch traced here: 49.9 us
  Pallas kernels  49.3 us (97%)
  local copies, waits for them, and re-layouts  0.61 us (1%)
    pallas_call x1, Pallas kernels, body(): pl.pallas_call(functools.partial(kernel, scale), out_shape=jax.ShapeDtype...  49.3 us

profile of v4, /device:TPU:6, one launch (start us, length us, event | category | flops | bytes accessed | tf_op | source)
XLA Modules:
  0.0 49.9 jit_solution(9088635408761275043)
XLA Ops:
  0.0 49.3 %latent_attend.1 = bf16[4,2,8,128]{3,2,1,0:T(8,128)(2,1)S(1)} custom-call(bf16[2,256,512]{2,1,0:T(8,128)(2,1)} %plat_hbm.1, bf16[2,64,256]{2,1,0:T(8,128)(2,1)} %prope_hbm.1, s32[1,2]{1,0:T(1,128)} %plen_hbm.1, s32[1,2]{1,0:T(1,128)} %dest_hbm.1, bf16[2,256,512]{2,1,0:T(8,128)(2,1)} %rlat_hbm.1, bf16[2,64,256]{2,1,0:T(8,128)(2,1)} %rrope_hbm.1, ...), custom_call_target="tpu_custom_call" | custom-call | tf_op jit(solution)/shard_map/latent_attend/pallas_call | solution.py:496
  49.3 0.6 %copy.15 = bf16[4,2,8,128]{3,2,1,0:T(8,128)(2,1)} copy(bf16[4,2,8,128]{3,2,1,0:T(8,128)(2,1)S(1)} %latent_attend.1) | data formatting | bytes 32768

commit v5 on v4

--- a/solution.py
+++ b/solution.py
@@ -62,22 +62,25 @@
     return out
 
 
-def attend(scale, gathered, keys, rope, length, offset, out_bf):
+def attend(scale, gathered, chunks, keys, rope, length, offset, out_bf):
+    n = len(chunks)
+    rows = [gathered[chunk] for chunk in chunks]
     q = jnp.concatenate(
-        [gathered[:, k * 16 : (k + 1) * 16, :].reshape(128, 128) for k in range(4)], axis=1
+        [jnp.concatenate([r[k * 16 : (k + 1) * 16] for r in rows], axis=0) for k in range(4)], axis=1
     )
-    ropes = gathered[:, 64:80, :].reshape(128, 128)[:, 0:64]
+    ropes = jnp.concatenate([r[64:80] for r in rows], axis=0)[:, 0:64]
     scores = lax.dot_general(q, keys, (((1,), (1,)), ((), ())), preferred_element_type=F32)
     scores = scale * (scores + jnp.dot(ropes, rope, preferred_element_type=F32))
-    live = offset + iota((128, 512), 1) < length
+    live = offset + iota((n * 16, 512), 1) < length
     scores = jnp.where(live, scores, NEG)
     top = jnp.max(scores, axis=-1, keepdims=True)
     weights = jnp.where(live, jnp.exp(scores - top), 0.0)
     total = jnp.sum(weights, axis=-1, keepdims=True)
     summed = jnp.dot(weights.astype(BF16), keys, preferred_element_type=F32)
-    summed = summed / jnp.maximum(total, 1.0)
-    out_bf[...] = summed.reshape(8, 16, 512).astype(BF16)
-    return top.reshape(8, 16, 1), total.reshape(8, 16, 1)
+    summed = (summed / jnp.maximum(total, 1.0)).astype(BF16)
+    for i, chunk in enumerate(chunks):
+        out_bf[chunk] = summed[i * 16 : (i + 1) * 16]
+    return top.reshape(n, 16, 1), total.reshape(n, 16, 1)
 
 
 def finish(blocks, stats, fresh_scores, fresh, vup):
@@ -332,6 +335,69 @@
             send(xa_copy(to, x))
         else:
             xr_a[x] = block
+    gather_mid(0)
+    for k in range(1, NX):
+        frm = (x + k) % NX
+        xa_copy(frm, frm).wait_recv()
+    block = xr_a[0].astype(F32)
+    for j in range(1, NX):
+        block = block + xr_a[j].astype(F32)
+    ropes_inc = [
+        jnp.concatenate([block[32 + 8 * r : 40 + 8 * r, 0:64], block[32 + 8 * r : 40 + 8 * r, 64:128]], axis=0)
+        for r in range(2)
+    ]
+    absorbed_inc = absorb(block[0:32].astype(BF16), kup)
+    gather_start(1, absorbed_inc, ropes_inc)
+
+    def out_copy(p, s, to, frm):
+        device = (g, to * 2 + c)
+        return remote(zs_bf.at[p, s, to], zr_bf.at[p, s, z], zo_ss.at[p, s, to], zo_rs.at[p, s, frm], device)
+
+    def stat_copy(p, to, frm):
+        device = (g, to * 2 + c)
+        return remote(zs_st.at[p, to], zr_st.at[p, z], zt_ss.at[p, to], zt_rs.at[p, frm], device)
+
+    FAR_FIRST = (4, 3, 5, 2, 6, 1, 7)
+
+    NEAR, REST = (0, 2, 6, 1, 7), (4, 3, 5)
+
+    def partials(p, s, lengths, offsets):
+        chunks = [(z + k) % NZ for k in offsets]
+        return attend(
+            scale, gathered.at[p, s], chunks, lat[p, s], rope[p, s], lengths[0, s], z * 512, zs_bf.at[p, s]
+        )
+
+    def share(p, s, offsets):
+        for k in offsets:
+            if k:
+                send(out_copy(p, s, (z + k) % NZ, z))
+            else:
+                zr_bf[p, s, z] = zs_bf[p, s, z]
+
+    def share_stats(p, offsets, fields):
+        rows = rows_of([fields[0][0], fields[1][0], fields[0][1], fields[1][1]])
+        for i, k in enumerate(offsets):
+            to = (z + k) % NZ
+            if k:
+                zs_st[p, to] = rows[i]
+                send(stat_copy(p, to, z))
+            else:
+                zr_st[p, z] = rows[i]
+
+    def collect(p):
+        for k in FAR_FIRST:
+            frm = (z + k) % NZ
+            for s in range(2):
+                out_copy(p, s, frm, frm).wait_recv()
+            stat_copy(p, frm, frm).wait_recv()
+
+    arrive(need_res)
+    for copy in sib_copies(0):
+        copy.wait_recv()
+    fields_res = []
+    for s in range(2):
+        gather_end(0, s)
+        fields_res.append(partials(0, s, rlen, NEAR + REST))
     for k in range(1, NY):
         frm = (y + k) % NY
         yb_copy(frm, frm).wait_recv()
@@ -345,20 +411,7 @@
             send(xb_copy(to, x))
         else:
             xr_b[x] = block
-    gather_mid(0)
-    for k in range(1, NX):
-        frm = (x + k) % NX
-        xa_copy(frm, frm).wait_recv()
-    block = xr_a[0].astype(F32)
-    for j in range(1, NX):
-        block = block + xr_a[j].astype(F32)
-    ropes_inc = [
-        jnp.concatenate([block[32 + 8 * r : 40 + 8 * r, 0:64], block[32 + 8 * r : 40 + 8 * r, 64:128]], axis=0)
-        for r in range(2)
-    ]
-    absorbed_inc = absorb(block[0:32].astype(BF16), kup)
-    gather_start(1, absorbed_inc, ropes_inc)
-
+    gather_mid(1)
     def da_copy(to):
         ref = dest_all.at[pl.ds(g * 2, 2)]
         return remote(ref, ref, da_ss, da_rs, (to, d))
@@ -367,6 +420,20 @@
     da_every = remote(dest_all.at[pl.ds(0, 62)], dest_all.at[pl.ds(0, 62)], da_ss, da_rs, along_y(1))
     all_sent.append(da_every)
 
+    arrive(need_inc)
+    for copy in sib_copies(1):
+        copy.wait_recv()
+    for offsets, kinds in ((NEAR, (0, 1)), (REST, (4, 5, 6, 7))):
+        fields_inc = []
+        for s in range(2):
+            for kind in kinds:
+                gather_in(1, s, kind).wait_recv()
+            fields_inc.append(partials(1, s, plen, offsets))
+            share(1, s, offsets)
+        share_stats(1, offsets, fields_inc)
+    share(0, 0, REST + NEAR)
+    share(0, 1, REST + NEAR)
+    share_stats(0, NEAR + REST, fields_res)
     for k in range(1, NX):
         frm = (x + k) % NX
         xb_copy(frm, frm).wait_recv()
@@ -386,59 +453,6 @@
         fresh_rope_inc.append([row[:, 0:64], row[:, 64:128]])
     scores_inc = new_scores(scale, absorbed_inc, ropes_inc, fresh_inc, fresh_rope_inc)
 
-    def out_copy(p, s, to, frm):
-        device = (g, to * 2 + c)
-        return remote(zs_bf.at[p, s, to], zr_bf.at[p, s, z], zo_ss.at[p, s, to], zo_rs.at[p, s, frm], device)
-
-    def stat_copy(p, to, frm):
-        device = (g, to * 2 + c)
-        return remote(zs_st.at[p, to], zr_st.at[p, z], zt_ss.at[p, to], zt_rs.at[p, frm], device)
-
-    FAR_FIRST = (4, 3, 5, 2, 6, 1, 7)
-
-    def partials(p, s, lengths):
-        return attend(
-            scale, gathered.at[p, s], lat[p, s], rope[p, s], lengths[0, s], z * 512, zs_bf.at[p, s]
-        )
-
-    def share(p, s):
-        for k in FAR_FIRST:
-            send(out_copy(p, s, (z + k) % NZ, z))
-        zr_bf[p, s, z] = zs_bf[p, s, z]
-
-    def share_stats(p, fields):
-        zs_st[p] = rows_of([fields[0][0], fields[1][0], fields[0][1], fields[1][1]])
-        for k in FAR_FIRST:
-            send(stat_copy(p, (z + k) % NZ, z))
-        zr_st[p, z] = zs_st[p, z]
-
-    def collect(p):
-        for k in FAR_FIRST:
-            frm = (z + k) % NZ
-            for s in range(2):
-                out_copy(p, s, frm, frm).wait_recv()
-            stat_copy(p, frm, frm).wait_recv()
-
-    arrive(need_res)
-    for copy in sib_copies(0):
-        copy.wait_recv()
-    fields_res = []
-    for s in range(2):
-        gather_end(0, s)
-        fields_res.append(partials(0, s, rlen))
-    gather_mid(1)
-    share(0, 0)
-    arrive(need_inc)
-    for copy in sib_copies(1):
-        copy.wait_recv()
-    fields_inc = []
-    for s in range(2):
-        gather_end(1, s)
-        fields_inc.append(partials(1, s, plen))
-        share(1, s)
-    share_stats(1, fields_inc)
-    share(0, 1)
-    share_stats(0, fields_res)
     arrive(need_vup)
     collect(1)
     out_inc = finish(zr_bf.at[1], zr_st.at[1], scores_inc, fresh_inc, vup)
@@ -456,7 +470,10 @@
         ret_send[to] = ret_block(to)
         remote(ret_send.at[to], ret_recv.at[g], ret_ss, ret_rs, (to, d)).start()
 
-    over_groups(ret_start)
+    for ky in FAR_FIRST + (0,):
+        for kx in (2, 1, 3, 0):
+            if kx or ky:
+                ret_start(((x + kx) % NX) * NY + (y + ky) % NY)
     ret_every = remote(ret_send.at[pl.ds(0, 31)], ret_recv.at[pl.ds(0, 31)], ret_ss, ret_rs, along_y(1))
     all_sent.append(ret_every)
     ret_recv[g] = ret_block(g)

time: 50.8 us -> 49.5 us (0.974)
  Pallas kernels: 49.3 us -> 48.2 us
    pallas_call x1, Pallas kernels: 49.3 us -> 48.2 us  [body(): pl.pallas_call(functools.partial(kernel, scale), out_shape=jax.ShapeDtype...]
where the time goes in v5:
time: 49.5 us; the launch traced here: 48.8 us
  Pallas kernels  48.2 us (97%)
  local copies, waits for them, and re-layouts  0.61 us (1%)
    pallas_call x1, Pallas kernels, body(): pl.pallas_call(functools.partial(kernel, scale), out_shape=jax.ShapeDtype...  48.2 us

profile of v5, /device:TPU:6, one launch (start us, length us, event | category | flops | bytes accessed | tf_op | source)
XLA Modules:
  0.0 48.8 jit_solution(7610235559168570896)
XLA Ops:
  0.0 48.2 %latent_attend.1 = bf16[4,2,8,128]{3,2,1,0:T(8,128)(2,1)S(1)} custom-call(bf16[2,256,512]{2,1,0:T(8,128)(2,1)} %plat_hbm.1, bf16[2,64,256]{2,1,0:T(8,128)(2,1)} %prope_hbm.1, s32[1,2]{1,0:T(1,128)} %plen_hbm.1, s32[1,2]{1,0:T(1,128)} %dest_hbm.1, bf16[2,256,512]{2,1,0:T(8,128)(2,1)} %rlat_hbm.1, bf16[2,64,256]{2,1,0:T(8,128)(2,1)} %rrope_hbm.1, ...), custom_call_target="tpu_custom_call" | custom-call | tf_op jit(solution)/shard_map/latent_attend/pallas_call | solution.py:513
  48.2 0.6 %copy.15 = bf16[4,2,8,128]{3,2,1,0:T(8,128)(2,1)} copy(bf16[4,2,8,128]{3,2,1,0:T(8,128)(2,1)S(1)} %latent_attend.1) | data formatting | bytes 32768

commit v6 on v5

--- a/solution.py
+++ b/solution.py
@@ -160,7 +160,7 @@
     def arrive(wanted):
         for load in wanted:
             load.wait()
-            waiting.remove(load)
+            waiting[:] = [other for other in waiting if other is not load]
 
     sent = []
 
@@ -391,13 +391,6 @@
                 out_copy(p, s, frm, frm).wait_recv()
             stat_copy(p, frm, frm).wait_recv()
 
-    arrive(need_res)
-    for copy in sib_copies(0):
-        copy.wait_recv()
-    fields_res = []
-    for s in range(2):
-        gather_end(0, s)
-        fields_res.append(partials(0, s, rlen, NEAR + REST))
     for k in range(1, NY):
         frm = (y + k) % NY
         yb_copy(frm, frm).wait_recv()
@@ -412,14 +405,6 @@
         else:
             xr_b[x] = block
     gather_mid(1)
-    def da_copy(to):
-        ref = dest_all.at[pl.ds(g * 2, 2)]
-        return remote(ref, ref, da_ss, da_rs, (to, d))
-
-    over_groups(lambda to: da_copy(to).start())
-    da_every = remote(dest_all.at[pl.ds(0, 62)], dest_all.at[pl.ds(0, 62)], da_ss, da_rs, along_y(1))
-    all_sent.append(da_every)
-
     arrive(need_inc)
     for copy in sib_copies(1):
         copy.wait_recv()
@@ -431,6 +416,14 @@
             fields_inc.append(partials(1, s, plen, offsets))
             share(1, s, offsets)
         share_stats(1, offsets, fields_inc)
+    arrive(need_res)
+    for copy in sib_copies(0):
+        copy.wait_recv()
+    fields_res = []
+    gather_end(0, 0)
+    fields_res.append(partials(0, 0, rlen, NEAR + REST))
+    gather_end(0, 1)
+    fields_res.append(partials(0, 1, rlen, NEAR + REST))
     share(0, 0, REST + NEAR)
     share(0, 1, REST + NEAR)
     share_stats(0, NEAR + REST, fields_res)
@@ -452,6 +445,14 @@
         row = block[16 + 8 * r : 17 + 8 * r]
         fresh_rope_inc.append([row[:, 0:64], row[:, 64:128]])
     scores_inc = new_scores(scale, absorbed_inc, ropes_inc, fresh_inc, fresh_rope_inc)
+
+    def da_copy(to):
+        ref = dest_all.at[pl.ds(g * 2, 2)]
+        return remote(ref, ref, da_ss, da_rs, (to, d))
+
+    over_groups(lambda to: da_copy(to).start())
+    da_every = remote(dest_all.at[pl.ds(0, 62)], dest_all.at[pl.ds(0, 62)], da_ss, da_rs, along_y(1))
+    all_sent.append(da_every)
 
     arrive(need_vup)
     collect(1)

time: 49.5 us -> 49 us (0.990)
  Pallas kernels: 48.2 us -> 47.7 us
where the time goes in v6:
time: 49 us; the launch traced here: 48.3 us
  Pallas kernels  47.7 us (97%)
  local copies, waits for them, and re-layouts  0.61 us (1%)
    pallas_call x1, Pallas kernels, body(): pl.pallas_call(functools.partial(kernel, scale), out_shape=jax.ShapeDtype...  47.7 us

profile of v6, /device:TPU:6, one launch (start us, length us, event | category | flops | bytes accessed | tf_op | source)
XLA Modules:
  0.0 48.3 jit_solution(13470439514037733110)
XLA Ops:
  0.0 47.7 %latent_attend.1 = bf16[4,2,8,128]{3,2,1,0:T(8,128)(2,1)S(1)} custom-call(bf16[2,256,512]{2,1,0:T(8,128)(2,1)} %plat_hbm.1, bf16[2,64,256]{2,1,0:T(8,128)(2,1)} %prope_hbm.1, s32[1,2]{1,0:T(1,128)} %plen_hbm.1, s32[1,2]{1,0:T(1,128)} %dest_hbm.1, bf16[2,256,512]{2,1,0:T(8,128)(2,1)} %rlat_hbm.1, bf16[2,64,256]{2,1,0:T(8,128)(2,1)} %rrope_hbm.1, ...), custom_call_target="tpu_custom_call" | custom-call | tf_op jit(solution)/shard_map/latent_attend/pallas_call | solution.py:514
  47.7 0.6 %copy.15 = bf16[4,2,8,128]{3,2,1,0:T(8,128)(2,1)} copy(bf16[4,2,8,128]{3,2,1,0:T(8,128)(2,1)S(1)} %latent_attend.1) | data formatting | bytes 32768

commit v7 on v6

--- a/solution.py
+++ b/solution.py
@@ -132,8 +132,8 @@
     sibling = (g, z * 2 + 1 - c)
 
     barrier = pltpu.get_barrier_semaphore()
-    peers = [along_y(k) for k in range(1, NY)] + [along_x(k) for k in range(1, NX)]
-    peers += [sibling] + [along_z(k) for k in range(1, NZ)]
+    peers = [along_y(k) for k in (4, 3, 5, 2, 6)] + [along_x(2)] + [along_z(k) for k in (2, -2)]
+    peers += [along_y(k) for k in (1, 7)] + [along_x(k) for k in (1, 3)] + [along_z(k) for k in (1, -1)] + [sibling]
     for peer in peers:
         pl.semaphore_signal(barrier, inc=1, device_id=peer, device_id_type=MESH)
 

time: 49 us -> 49.1 us (level); the launches traced: 48.3 us -> 48.9 us
  Pallas kernels: 47.7 us -> 48.3 us
    pallas_call x1, Pallas kernels: 47.7 us -> 48.3 us  [body(): pl.pallas_call(functools.partial(kernel, scale), out_shape=jax.ShapeDtype...]
where the time goes in v7:
time: 49.1 us; the launch traced here: 48.9 us
  Pallas kernels  48.3 us (98%)
  local copies, waits for them, and re-layouts  0.61 us (1%)
    pallas_call x1, Pallas kernels, body(): pl.pallas_call(functools.partial(kernel, scale), out_shape=jax.ShapeDtype...  48.3 us

profile of v7, /device:TPU:6, one launch (start us, length us, event | category | flops | bytes accessed | tf_op | source)
XLA Modules:
  0.0 48.9 jit_solution(10382143473927298300)
XLA Ops:
  0.0 48.3 %latent_attend.1 = bf16[4,2,8,128]{3,2,1,0:T(8,128)(2,1)S(1)} custom-call(bf16[2,256,512]{2,1,0:T(8,128)(2,1)} %plat_hbm.1, bf16[2,64,256]{2,1,0:T(8,128)(2,1)} %prope_hbm.1, s32[1,2]{1,0:T(1,128)} %plen_hbm.1, s32[1,2]{1,0:T(1,128)} %dest_hbm.1, bf16[2,256,512]{2,1,0:T(8,128)(2,1)} %rlat_hbm.1, bf16[2,64,256]{2,1,0:T(8,128)(2,1)} %rrope_hbm.1, ...), custom_call_target="tpu_custom_call" | custom-call | tf_op jit(solution)/shard_map/latent_attend/pallas_call | solution.py:514
  48.3 0.6 %copy.15 = bf16[4,2,8,128]{3,2,1,0:T(8,128)(2,1)} copy(bf16[4,2,8,128]{3,2,1,0:T(8,128)(2,1)S(1)} %latent_attend.1) | data formatting | bytes 32768
